TPU v7x, 32 devices: a whole 2x2x4 slice. The times are simulated.
32 devices in a mesh: exp: 8 (over z, x), rep: 4 (over y, core).
Axes of the slice: x: 2, y: 2, z: 4, core: 2. Of those that a mesh axis runs over, the one named last changes fastest.
Arguments:
- images: bfloat16 [64, 256, 1024], P(('exp', 'rep')), may hold values from -12 to 12
- router: float32 [1024, 32], P(('exp', 'rep')), may hold values from -4 to 4
- w_in: bfloat16 [32, 1024, 2560], P(('exp', 'rep')), may hold values from -0.1875 to 0.1875
- w_out: bfloat16 [32, 2560, 1024], P(('exp', 'rep')), may hold values from -0.125 to 0.125
- out_grad: bfloat16 [64, 256, 1024], P(('exp', 'rep')), may hold values from -6 to 6
Outputs:
- images_grad: bfloat16 [64, 256, 1024], P(('exp', 'rep'))
- w_in_grad: bfloat16 [32, 1024, 2560], P(('exp', 'rep'))
- w_out_grad: bfloat16 [32, 2560, 1024], P(('exp', 'rep'))
- router_grad: float32 [1024, 32], P(('exp', 'rep'))
All inputs are finite; a program needn't handle non-finite values.
Results may differ from a plain program's by a relative error of at most 0.012.
The roundings to bfloat16 on the way count: a program that leaves them out, or rounds other values in their place, can miss the bound.
Values may be sent and summed in bfloat16 or wider, within the bound.
A program may use at most 128 MiB of HBM per device.

v0:
```python
import jax
import jax.numpy as jnp
from jax import lax
from jax.sharding import PartitionSpec as P

LOGIT_SCALE = 2.0
EPS = 1e-06
SQRT_HALF = 0.7071067811865476
INV_ROOT = 0.3989422804014327


def gelu_parts(pre_value):
    cumulative = 0.5 * (1.0 + lax.erf(pre_value * SQRT_HALF))
    gelu_slope = cumulative + pre_value * jnp.exp(-0.5 * pre_value * pre_value) * INV_ROOT
    return (pre_value * cumulative, gelu_slope)


def contract_last(left_side, right_side):
    return lax.dot_general(
        left_side, right_side, (((1,), (1,)), ((), ())), preferred_element_type=jnp.float32
    )


def contract_first(left_side, right_side):
    return lax.dot_general(
        left_side, right_side, (((0,), (0,)), ((), ())), preferred_element_type=jnp.float32
    )


def expert_pass(slot_rows, slot_grads, weight_in, weight_out):
    pre_act = jnp.dot(slot_rows, weight_in, preferred_element_type=jnp.float32)
    activated, gelu_slope = gelu_parts(pre_act)
    hidden = activated.astype(jnp.bfloat16)
    slot_out = jnp.dot(hidden, weight_out, preferred_element_type=jnp.float32).astype(jnp.bfloat16)
    hidden_grad = contract_last(slot_grads, weight_out)
    pre_grad = (hidden_grad * gelu_slope).astype(jnp.bfloat16)
    grad_out = contract_first(hidden, slot_grads).astype(jnp.bfloat16)
    grad_in = contract_first(slot_rows, pre_grad).astype(jnp.bfloat16)
    slot_dx = contract_last(pre_grad, weight_in).astype(jnp.bfloat16)
    return (slot_out, slot_dx, grad_in, grad_out)


def per_device(images, router, w_in, w_out, out_grad):
    model_width = images.shape[2]
    router_whole = lax.all_gather(router, ("exp", "rep"), axis=0, tiled=True)
    inv_norm = lax.rsqrt(jnp.sum(router_whole * router_whole, axis=0) + EPS)
    router_low = (router_whole * inv_norm).astype(jnp.bfloat16)
    logits = LOGIT_SCALE * jnp.einsum(
        "btd,de->bte", images, router_low, preferred_element_type=jnp.float32
    )
    dispatch = jax.nn.softmax(logits, axis=1)
    combine = jax.nn.softmax(logits, axis=2)
    dispatch_low = dispatch.astype(jnp.bfloat16)
    combine_low = combine.astype(jnp.bfloat16)
    slot_in = jnp.einsum(
        "bte,btd->bed", dispatch_low, images, preferred_element_type=jnp.float32
    ).astype(jnp.bfloat16)
    slot_grad = jnp.einsum(
        "bte,btd->bed", combine_low, out_grad, preferred_element_type=jnp.float32
    ).astype(jnp.bfloat16)
    paired = jnp.stack((slot_in, slot_grad), axis=0)
    arrived = lax.all_to_all(paired, ("exp", "rep"), split_axis=2, concat_axis=1, tiled=True)
    arrived = arrived.reshape(2, -1, model_width)
    slot_out, slot_dx, grad_in, grad_out = expert_pass(arrived[0], arrived[1], w_in[0], w_out[0])
    results = jnp.stack((slot_out, slot_dx), axis=0)
    returned = lax.all_to_all(
        results[:, :, None, :], ("exp", "rep"), split_axis=1, concat_axis=2, tiled=True
    )
    combine_grad = jnp.einsum(
        "btd,bed->bte", out_grad, returned[0], preferred_element_type=jnp.float32
    )
    grad_combine = combine * (combine_grad - jnp.sum(combine * combine_grad, axis=2, keepdims=True))
    dispatch_grad = jnp.einsum(
        "btd,bed->bte", images, returned[1], preferred_element_type=jnp.float32
    )
    grad_dispatch = dispatch * (
        dispatch_grad - jnp.sum(dispatch * dispatch_grad, axis=1, keepdims=True)
    )
    logit_grad = (LOGIT_SCALE * (grad_combine + grad_dispatch)).astype(jnp.bfloat16)
    images_grad = (
        jnp.einsum("bte,bed->btd", dispatch_low, returned[1], preferred_element_type=jnp.float32)
        + jnp.einsum("bte,de->btd", logit_grad, router_low, preferred_element_type=jnp.float32)
    ).astype(jnp.bfloat16)
    hat_rows = lax.psum_scatter(
        jnp.einsum("btd,bte->de", images, logit_grad, preferred_element_type=jnp.float32),
        ("exp", "rep"),
        scatter_dimension=0,
        tiled=True,
    )
    own_hat = router * inv_norm
    own_low = lax.optimization_barrier(own_hat.astype(jnp.bfloat16)).astype(jnp.float32)
    moment = lax.psum(jnp.sum(own_low * hat_rows, axis=0), ("exp", "rep"))
    router_grad = (hat_rows - own_hat * moment) * inv_norm
    return (images_grad, grad_in[None], grad_out[None], router_grad)


def solution(mesh):
    in_specs = (
        P(("exp", "rep"), None, None),
        P(("exp", "rep"), None),
        P(("exp", "rep"), None, None),
        P(("exp", "rep"), None, None),
        P(("exp", "rep"), None, None),
    )
    out_specs = (
        P(("exp", "rep"), None, None),
        P(("exp", "rep"), None, None),
        P(("exp", "rep"), None, None),
        P(("exp", "rep"), None),
    )
    return jax.shard_map(
        per_device, mesh=mesh, in_specs=in_specs, out_specs=out_specs, check_vma=False
    )
```

profile of v0, /device:TPU:0, one launch (start us, length us, event | category | flops | bytes accessed | tf_op | source)
XLA Modules:
  0.0 279.7 jit_solution(15479096234081932970)
XLA Ops:
  7.2 0.0 copy-start
  7.2 0.0 copy-start.7
  7.2 45.1 %all_gather.3 = f32[1024,32]{1,0:T(8,128)S(1)} all-gather(f32[32,32]{1,0:T(8,128)} %param.6), channel_id=1, replica_groups=mesh['exp'=8,'rep'=4] {'exp','rep'}, dimensions={0}, use_global_device_ids=true | all-gather | bytes 135168 | tf_op jit(solution)/shard_map/all_gather | solution.py:45
  52.3 0.2 multiply_reduce_fusion
  52.5 0.2 copy.40
  52.7 0.0 copy-done
  52.7 0.0 copy-start.13
  52.7 0.4 fusion.44
  53.1 0.0 copy-start.3
  53.1 0.7 fusion.70
  53.8 0.1 fusion.69
  54.0 0.0 copy-start.9
  54.0 0.0 copy-start.6
  54.0 0.3 fusion.26
  54.3 0.1 copy-done.11
  54.4 1.5 fusion.27
  56.0 1.0 copy.41
  56.9 0.0 copy-done.3
  56.9 2.6 all-to-all-start
  59.5 0.0 copy-done.7
  59.5 0.1 copy.44
  59.6 10.5 %all-to-all-done = bf16[2,2,32,1024]{3,1,0,2:T(2,128)(2,1)S(1)} async-done(((bf16[2,2,32,1024]{3,1,0,2:T(2,128)(2,1)}), bf16[2,2,32,1024]{3,1,0,2:T(2,128)(2,1)S(1)}, u32[]{:S(2)}, u32[]{:S(2)}) %all-to-all-start) | async-done | bytes 262176 | tf_op jit(solution)/shard_map/all_to_all | solution.py:62
  70.1 0.0 copy-done.9
  70.1 0.2 fusion.68
  70.3 0.1 squeeze.19
  70.4 0.1 squeeze.22
  70.4 0.0 copy-start.1
  70.5 0.0 slice-start
  70.5 3.6 %fusion.10 = f32[64,2560]{1,0:T(8,128)S(1)} fusion(bf16[64,1024]{1,0:T(8,128)(2,1)S(1)} %squeeze.19, bf16[1,1024,2560]{2,1,0:T(8,128)(2,1)} %param.7), kind=kOutput, calls=%fused_computation.12 | convolution fusion | flops 335544320 | bytes 6029312 | tf_op jit(solution)/shard_map/dot_general | solution.py:31
  74.1 0.4 copy-done.1
  74.5 1.0 fusion.28
  75.5 1.7 fusion.17
  77.2 0.0 slice-done
  77.2 0.0 slice-done.1
  77.3 1.7 fusion.31
  79.0 1.0 copy.42
  80.0 3.3 %all-to-all-start.1 = ((bf16[2,64,1,1024]{3,0,2,1:T(2,128)(2,1)}), bf16[2,64,1,1024]{3,0,2,1:T(2,128)(2,1)}, u32[]{:S(2)}, u32[]{:S(2)}) async-start(bf16[2,64,1,1024]{3,0,2,1:T(2,128)(2,1)} %copy.42), calls=%async_computation.1 | async-start | bytes 524288 | tf_op jit(solution)/shard_map/all_to_all | solution.py:66
  83.3 0.0 reduce-scatter.4.cloned.1.call-start
  83.3 0.0 copy-done.13
  83.3 0.7 multiply_convert_fusion.2
  84.0 3.9 %fusion.12 = bf16[1,1024,2560]{2,1,0:T(8,128)(2,1)} fusion(bf16[64,1024]{1,0:T(8,128)(2,1)S(1)} %squeeze.19, bf16[64,2560]{1,0:T(8,128)(2,1)S(1)} %fusion.17), kind=kOutput, calls=%fused_computation.14 | convolution fusion | flops 338165760 | bytes 5701632 | tf_op jit(solution)/shard_map/dot_general | solution.py:25
  87.9 3.9 %fusion.13 = bf16[1,2560,1024]{2,1,0:T(8,128)(2,1)} fusion(bf16[64,1024]{1,0:T(8,128)(2,1)S(1)} %squeeze.22, f32[64,2560]{1,0:T(8,128)S(1)} %fusion.10), kind=kOutput, calls=%fused_computation.15 | convolution fusion | flops 338984960 | bytes 6029312 | tf_op jit(solution)/shard_map/dot_general | solution.py:25
  91.9 2.0 all-to-all-done.1
  93.9 1.0 copy.49
  94.9 0.0 copy-done.2
  94.9 0.4 convolution_bitcast_fusion.2
  95.3 0.4 convolution_bitcast_fusion.1
  95.7 0.0 copy-done.8
  95.8 0.0 copy-done.12
  95.8 0.3 fusion.43
  96.1 0.0 copy-done.6
  96.1 0.0 copy-done.10
  96.1 0.3 convolution_bitcast_fusion
  96.4 1.0 copy.46
  97.4 0.0 copy-done.5
  97.4 0.0 reduce-scatter.4.cloned.1.call-update
  97.5 1.5 fusion.54
  99.0 131.7 %reduce-scatter.4.cloned.1.call-done = f32[32,32]{1,0:T(8,128)} async-done(((f32[1024,32]{1,0:T(8,128)}), f32[32,32]{1,0:T(8,128)}) %reduce-scatter.4.cloned.1.call-update) | async-done | bytes 4112
  230.7 0.8 copy.47
  231.4 0.8 multiply_reduce_fusion.3
  232.3 2.4 add_convert_fusion
  234.7 36.8 %psum.7 = f32[32]{0:T(128)S(1)} all-reduce(f32[32]{0:T(128)S(1)} %multiply_reduce_fusion.3), channel_id=1, replica_groups=mesh['exp'=8,'rep'=4] {'exp','rep'}, use_global_device_ids=true, to_apply=%region_9.0 | all-reduce | flops 32 | bytes 256 | tf_op jit(solution)/shard_map/psum | solution.py:92
  271.5 0.7 subtract_multiply_fusion
  272.2 0.7 copy.45
  (13 shorter events, 0.1 us)
Async XLA Ops:
  7.2 45.5 %copy-start = (bf16[2,256,1024]{2,1,0:T(8,128)(2,1)S(1)}, bf16[2,256,1024]{2,1,0:T(8,128)(2,1)}, u32[]{:S(2)}) copy-start(bf16[2,256,1024]{2,1,0:T(8,128)(2,1)} %param.5) | copy-start | bytes 3145732
  7.2 52.4 %copy-start.7 = (f32[32,32]{1,0:T(8,128)S(1)}, f32[32,32]{1,0:T(8,128)}, u32[]{:S(2)}) copy-start(f32[32,32]{1,0:T(8,128)} %param.6) | copy-start | bytes 12292
  52.7 30.7 %copy-start.13 = (f32[32]{0:T(128)}, f32[32]{0:T(128)S(1)}, u32[]{:S(2)}) copy-start(f32[32]{0:T(128)S(1)} %add_rsqrt_fusion) | copy-start | bytes 388
  53.1 3.9 %copy-start.3 = (f32[2,256,32]{1,2,0:T(8,128)}, f32[2,256,32]{1,2,0:T(8,128)S(1)}, u32[]{:S(2)}) copy-start(f32[2,256,32]{1,2,0:T(8,128)S(1)} %fusion.44) | copy-start | bytes 196612
  53.8 0.6 copy-start.11
  54.0 16.2 %copy-start.9 = (f32[2,256]{1,0:T(2,128)}, f32[2,256]{1,0:T(2,128)S(1)}, u32[]{:S(2)}) copy-start(f32[2,256]{1,0:T(2,128)S(1)} %get-tuple-element.30) | copy-start | bytes 6148
  54.0 42.1 %copy-start.6 = (f32[2,256,32]{1,2,0:T(8,128)}, f32[2,256,32]{1,2,0:T(8,128)S(1)}, u32[]{:S(2)}) copy-start(f32[2,256,32]{1,2,0:T(8,128)S(1)} %get-tuple-element.31) | copy-start | bytes 196612
  56.9 13.2 %all-to-all-start = ((bf16[2,2,32,1024]{3,1,0,2:T(2,128)(2,1)}), bf16[2,2,32,1024]{3,1,0,2:T(2,128)(2,1)S(1)}, u32[]{:S(2)}, u32[]{:S(2)}) async-start(bf16[2,2,32,1024]{3,1,0,2:T(2,128)(2,1)} %copy.41), calls=%async_computation | async-start | bytes 524288 | tf_op jit(solution)/shard_map/all_to_all | solution.py:62
  70.4 4.0 %copy-start.1 = (bf16[1,2560,1024]{2,1,0:T(8,128)(2,1)S(1)}, bf16[1,2560,1024]{2,1,0:T(8,128)(2,1)}, u32[]{:S(2)}) copy-start(bf16[1,2560,1024]{2,1,0:T(8,128)(2,1)} %param.8) | copy-start | bytes 15728644
  70.5 6.8 %slice-start = ((s8[5242880]{0:T(1024)(128)(4,1)}), s8[4194304]{0:T(1024)(128)(4,1)S(1)}, s32[]{:S(2)}) async-start(s8[5242880]{0:T(1024)(128)(4,1)} %bitcast.86), calls=%async_computation.4 | async-start | bytes 8388608
  74.5 2.8 slice-start.1
  80.0 13.9 %all-to-all-start.1 = ((bf16[2,64,1,1024]{3,0,2,1:T(2,128)(2,1)}), bf16[2,64,1,1024]{3,0,2,1:T(2,128)(2,1)}, u32[]{:S(2)}, u32[]{:S(2)}) async-start(bf16[2,64,1,1024]{3,0,2,1:T(2,128)(2,1)} %copy.42), calls=%async_computation.1 | async-start | bytes 524288 | tf_op jit(solution)/shard_map/all_to_all | solution.py:66
  83.3 147.4 %reduce-scatter.4.cloned.1.call-start = ((), (), s32[]{:S(2)}) async-start(), calls=%async_computation.3 | async-start | bytes 540672
  84.0 10.9 %copy-start.2 = (bf16[2,256,1024]{2,1,0:T(8,128)(2,1)S(1)}, bf16[2,256,1024]{2,1,0:T(8,128)(2,1)}, u32[]{:S(2)}) copy-start(bf16[2,256,1024]{2,1,0:T(8,128)(2,1)} %param.9) | copy-start | bytes 3145732
  87.9 7.8 %copy-start.8 = (f32[2,256,32]{1,2,0:T(8,128)S(1)}, f32[2,256,32]{1,2,0:T(8,128)}, u32[]{:S(2)}) copy-start(f32[2,256,32]{1,2,0:T(8,128)} %get-tuple-element.33) | copy-start | bytes 196612
  87.9 7.8 %copy-start.12 = (f32[2,32]{1,0:T(2,128)S(1)}, f32[2,32]{1,0:T(2,128)}, u32[]{:S(2)}) copy-start(f32[2,32]{1,0:T(2,128)} %copy-done.11) | copy-start | bytes 772
  87.9 8.2 %copy-start.10 = (f32[2,256]{1,0:T(2,128)S(1)}, f32[2,256]{1,0:T(2,128)}, u32[]{:S(2)}) copy-start(f32[2,256]{1,0:T(2,128)} %copy-done.9) | copy-start | bytes 6148
  95.3 2.1 copy-start.5
  96.1 1.3 copy-start.4
Sparse Core Ops, SparseCore 0:
  97.6 133.0 reduce-scatter.3
where the time goes:
time: 281 us; the launch traced here: 280 us
  waiting for transfers between devices  144 us (51%)
  blocking collectives  82 us (29%)
  matrix products  23.2 us (8%)
  between operations  14.3 us (5%)
  local copies, waits for them, and re-layouts  6.55 us (2%)
  starting transfers between devices  5.94 us (2%)
  other arithmetic  3.6 us (1%)
    unnamed x2, waiting for transfers between devices  132 us
    all_gather x1, blocking collectives, per_device(): router_whole = lax.all_gather(router, ('exp', 'rep'), axis=0, tiled=True)  45.1 us
    psum x1, blocking collectives, per_device(): moment = lax.psum(jnp.sum(own_low * hat_rows, axis=0), ('exp', 'rep'))  36.8 us
    all_to_all x1, waiting for transfers between devices, per_device(): lax.all_to_all(paired, ('exp', 'rep'), split_axis=2, concat_axis=1, tiled...  10.5 us
    dot_general x2, matrix products, contract_first(): lax.dot_general(left_side, right_side, (((0,), (0,)), ((), ())), preferre...  7.84 us
  transfers between devices with their start and end apart: 3, of which 3 were waited for; matrix products, arithmetic and copies ran while one was open for 4% of the time, Pallas kernels for 0%

commit v1 on v0

--- a/solution.py
+++ b/solution.py
@@ -42,7 +42,14 @@
 
 def per_device(images, router, w_in, w_out, out_grad):
     model_width = images.shape[2]
-    router_whole = lax.all_gather(router, ("exp", "rep"), axis=0, tiled=True)
+    devices = lax.axis_size(("exp", "rep"))
+    router_whole = lax.all_to_all(
+        jnp.broadcast_to(router[None], (devices,) + router.shape),
+        ("exp", "rep"),
+        split_axis=0,
+        concat_axis=0,
+        tiled=True,
+    ).reshape(model_width, -1)
     inv_norm = lax.rsqrt(jnp.sum(router_whole * router_whole, axis=0) + EPS)
     router_low = (router_whole * inv_norm).astype(jnp.bfloat16)
     logits = LOGIT_SCALE * jnp.einsum(
@@ -81,15 +88,21 @@
         jnp.einsum("bte,bed->btd", dispatch_low, returned[1], preferred_element_type=jnp.float32)
         + jnp.einsum("bte,de->btd", logit_grad, router_low, preferred_element_type=jnp.float32)
     ).astype(jnp.bfloat16)
-    hat_rows = lax.psum_scatter(
-        jnp.einsum("btd,bte->de", images, logit_grad, preferred_element_type=jnp.float32),
-        ("exp", "rep"),
-        scatter_dimension=0,
-        tiled=True,
+    hat_part = jnp.einsum("btd,bte->de", images, logit_grad, preferred_element_type=jnp.float32)
+    moment_part = jnp.sum(router_low.astype(jnp.float32) * hat_part, axis=0)
+    packed = jnp.concatenate(
+        (
+            hat_part.reshape((devices,) + router.shape),
+            jnp.broadcast_to(moment_part, (devices, 1) + moment_part.shape),
+        ),
+        axis=1,
     )
+    summed = jnp.sum(
+        lax.all_to_all(packed, ("exp", "rep"), split_axis=0, concat_axis=0, tiled=True), axis=0
+    )
+    hat_rows = summed[:-1]
+    moment = summed[-1]
     own_hat = router * inv_norm
-    own_low = lax.optimization_barrier(own_hat.astype(jnp.bfloat16)).astype(jnp.float32)
-    moment = lax.psum(jnp.sum(own_low * hat_rows, axis=0), ("exp", "rep"))
     router_grad = (hat_rows - own_hat * moment) * inv_norm
     return (images_grad, grad_in[None], grad_out[None], router_grad)
 

time: 281 us -> 88.6 us (0.32)
  waiting for transfers between devices: 144 us -> 8.57 us
  blocking collectives: 82 us -> 27.7 us
  between operations: 14.3 us -> 0.96 us
  local copies, waits for them, and re-layouts: 6.55 us -> 11.3 us
  matrix products: 23.2 us -> 27.1 us
    unnamed x2 -> x0, waiting for transfers between devices: 132 us -> none
    all_gather x1 -> x0, blocking collectives: 45.1 us -> none  [per_device(): router_whole = lax.all_gather(router, ('exp', 'rep'), axis=0, tiled=True)]
    psum x1 -> x0, blocking collectives: 36.8 us -> none  [per_device(): moment = lax.psum(jnp.sum(own_low * hat_rows, axis=0), ('exp', 'rep'))]
    all_to_all x0 -> x2, blocking collectives: none -> 27.7 us  [the longest x1 15.3 us: per_device(): lax.all_to_all(jnp.broadcast_to(router[None], (devices,) + router.shape),...]
    all_to_all x1, waiting for transfers between devices: 10.5 us -> 6.02 us  [per_device(): lax.all_to_all(packed, ('exp', 'rep'), split_axis=0, concat_axis=0, tiled...]
    dot_general x1, matrix products: 1.02 us -> 4.06 us  [expert_pass(): jnp.dot(hidden, weight_out, preferred_element_type=jnp.float32)]
  transfers between devices with their start and end apart: 3 -> 2, of which waited for: 3 -> 2; matrix products, arithmetic and copies ran while one was open for 4% -> 12% of each run, Pallas kernels for 0% -> 0%
where the time goes in v1:
time: 88.6 us; the launch traced here: 88 us
  blocking collectives  27.7 us (31%)
  matrix products  27.1 us (31%)
  local copies, waits for them, and re-layouts  11.3 us (13%)
  waiting for transfers between devices  8.57 us (10%)
  starting transfers between devices  6.54 us (7%)
  other arithmetic  5.87 us (7%)
  between operations  0.96 us (1%)
    all_to_all x1, blocking collectives, per_device(): lax.all_to_all(jnp.broadcast_to(router[None], (devices,) + router.shape),...  15.3 us
    all_to_all x1, blocking collectives, per_device(): lax.all_to_all(paired, ('exp', 'rep'), split_axis=2, concat_axis=1, tiled...  12.4 us
    dot_general x2, matrix products, contract_first(): lax.dot_general(left_side, right_side, (((0,), (0,)), ((), ())), preferre...  7.83 us
    all_to_all x1, waiting for transfers between devices, per_device(): lax.all_to_all(packed, ('exp', 'rep'), split_axis=0, concat_axis=0, tiled...  6.02 us
    unnamed x31, local copies, waits for them, and re-layouts  5.1 us
    dot_general x1, matrix products, expert_pass(): jnp.dot(hidden, weight_out, preferred_element_type=jnp.float32)  4.06 us
    dot_general x1, matrix products, expert_pass(): pre_act = jnp.dot(slot_rows, weight_in, preferred_element_type=jnp.float32)  3.65 us
    all_to_all x1, starting transfers between devices, per_device(): lax.all_to_all(results[:, :, None, :], ('exp', 'rep'), split_axis=1, conc...  3.49 us
  transfers between devices with their start and end apart: 2, of which 2 were waited for; matrix products, arithmetic and copies ran while one was open for 12% of the time, Pallas kernels for 0%

profile of v1, /device:TPU:0, one launch (start us, length us, event | category | flops | bytes accessed | tf_op | source)
XLA Modules:
  0.0 88.0 jit_solution(14896704116222145181)
XLA Ops:
  0.6 0.0 copy-start
  0.6 0.0 copy-start.1
  0.7 0.9 %copy.23 = f32[32,32]{0,1:T(8,128)S(1)} copy(f32[32,32]{1,0:T(8,128)} %param.6) | data formatting | bytes 8192 | tf_op args[1]
  1.6 0.1 broadcast_bitcast_fusion
  1.7 0.3 reshape.40
  1.9 15.3 %all_to_all.40 = f32[32,1,1024]{2,1,0:T(1,128)S(1)} all-to-all(f32[32,1,1024]{2,1,0:T(1,128)S(1)} %reshape.40), channel_id=1, replica_groups=mesh['exp'=8,'rep'=4] {'exp','rep'}, dimensions={0} | all-to-all | bytes 262144 | tf_op jit(solution)/shard_map/all_to_all | solution.py:46
  17.3 0.5 broadcast.32
  17.8 0.9 %reduce.3 = f32[32,1024]{1,0:T(8,128)S(1)} reduce(f32[32,1,1024]{2,1,0:T(1,128)S(1)} %all_to_all.40, f32[]{:T(128)} %broadcast.32), dimensions={1}, to_apply=%all_to_all.28.reduce_sub_computation | reduce | bytes 262148 | tf_op jit(solution)/shard_map/all_to_all | solution.py:46
  18.7 0.2 reshape.41
  18.9 0.2 multiply_reduce_fusion
  19.1 0.0 copy-start.6
  19.1 0.3 copy.24
  19.4 0.2 reshape.35
  19.6 0.0 copy-done.6
  19.7 0.1 multiply_convert_fusion.1
  19.7 0.0 copy-done
  19.7 0.4 fusion.44
  20.2 0.7 fusion.70
  20.9 0.6 fusion.69
  21.5 0.3 fusion.26
  21.9 0.0 copy-done.5
  21.9 0.0 copy-done.1
  21.9 0.3 fusion.27
  22.2 0.3 copy.25
  22.5 12.4 %all_to_all.41 = bf16[2,2,32,1024]{3,1,0,2:T(2,128)(2,1)S(1)} all-to-all(bf16[2,2,32,1024]{3,1,0,2:T(2,128)(2,1)S(1)} %copy.25), channel_id=1, replica_groups=mesh['exp'=8,'rep'=4] {'exp','rep'}, dimensions={2} | all-to-all | bytes 524288 | tf_op jit(solution)/shard_map/all_to_all | solution.py:69
  34.9 0.2 fusion.68
  35.0 0.1 squeeze.19
  35.1 0.0 copy-done.3
  35.1 0.0 slice-start
  35.1 0.1 squeeze.22
  35.2 0.0 slice-start.1
  35.2 0.0 slice-start.2
  35.2 3.6 %fusion.10 = f32[64,2560]{1,0:T(8,128)S(1)} fusion(bf16[64,1024]{1,0:T(8,128)(2,1)S(1)} %squeeze.19, bf16[1,1024,2560]{2,1,0:T(8,128)(2,1)} %param.7), kind=kOutput, calls=%fused_computation.12 | convolution fusion | flops 335544320 | bytes 6029312 | tf_op jit(solution)/shard_map/dot_general | solution.py:31
  38.9 0.0 slice-start.3
  38.9 4.1 %fusion.28 = bf16[1,64,1024]{2,1,0:T(8,128)(2,1)S(1)} fusion(bf16[1,2560,1024]{2,1,0:T(8,128)(2,1)} %param.8, f32[64,2560]{1,0:T(8,128)S(1)} %fusion.10), kind=kOutput, calls=%fused_computation.26 | convolution fusion | flops 336429056 | bytes 6029312 | tf_op jit(solution)/shard_map/dot_general | solution.py:34
  43.0 1.7 %fusion.17 = bf16[64,2560]{1,0:T(8,128)(2,1)S(1)} fusion(bf16[64,1024]{1,0:T(8,128)(2,1)S(1)} %squeeze.22, bf16[1,2560,1024]{2,1,0:T(8,128)(2,1)S(1)} %bitcast.99, f32[64,2560]{1,0:T(8,128)S(1)} %fusion.10), kind=kOutput, calls=%fused_computation.17 | convolution fusion | flops 337182720 | bytes 6356992 | tf_op jit(solution)/shard_map/dot_general | solution.py:19
  44.7 1.7 %fusion.31 = bf16[1,64,1024]{2,1,0:T(8,128)(2,1)S(1)} fusion(bf16[64,2560]{1,0:T(8,128)(2,1)S(1)} %fusion.17, bf16[1,1024,2560]{2,1,0:T(8,128)(2,1)S(1)} %bitcast.101), kind=kOutput, calls=%fused_computation.27 | convolution fusion | flops 335609856 | bytes 5701632 | tf_op jit(solution)/shard_map/dot_general | solution.py:19
  46.4 1.0 %copy.26 = bf16[2,64,1,1024]{3,0,2,1:T(2,128)(2,1)} copy(bf16[2,64,1,1024]{3,1,0,2:T(8,128)(2,1)S(1)} %maximum_bitcast_fusion) | data formatting | bytes 524288 | tf_op jit(solution)/shard_map/broadcast_in_dim | solution.py:74
  47.4 3.5 %all-to-all-start.2 = ((bf16[2,64,1,1024]{3,0,2,1:T(2,128)(2,1)}), bf16[2,64,1,1024]{3,0,2,1:T(2,128)(2,1)}, u32[]{:S(2)}, u32[]{:S(2)}) async-start(bf16[2,64,1,1024]{3,0,2,1:T(2,128)(2,1)} %copy.26), calls=%async_computation.2 | async-start | bytes 524288 | tf_op jit(solution)/shard_map/all_to_all | solution.py:73
  50.9 0.0 copy-start.2
  50.9 3.9 %fusion.12 = bf16[1,1024,2560]{2,1,0:T(8,128)(2,1)} fusion(bf16[64,1024]{1,0:T(8,128)(2,1)S(1)} %squeeze.19, bf16[64,2560]{1,0:T(8,128)(2,1)S(1)} %fusion.17), kind=kOutput, calls=%fused_computation.14 | convolution fusion | flops 338165760 | bytes 5701632 | tf_op jit(solution)/shard_map/dot_general | solution.py:25
  54.8 3.9 %fusion.13 = bf16[1,2560,1024]{2,1,0:T(8,128)(2,1)} fusion(bf16[64,1024]{1,0:T(8,128)(2,1)S(1)} %squeeze.22, f32[64,2560]{1,0:T(8,128)S(1)} %fusion.10), kind=kOutput, calls=%fused_computation.15 | convolution fusion | flops 338984960 | bytes 6029312 | tf_op jit(solution)/shard_map/dot_general | solution.py:25
  58.8 2.5 %all-to-all-done.2 = bf16[2,64,1,1024]{3,0,2,1:T(2,128)(2,1)} async-done(((bf16[2,64,1,1024]{3,0,2,1:T(2,128)(2,1)}), bf16[2,64,1,1024]{3,0,2,1:T(2,128)(2,1)}, u32[]{:S(2)}, u32[]{:S(2)}) %all-to-all-start.2) | async-done | bytes 262176 | tf_op jit(solution)/shard_map/all_to_all | solution.py:73
  61.3 1.0 %copy.36 = bf16[2,32,2,1,1024]{4,1,2,3,0:T(8,128)(2,1)S(1)} copy(bf16[2,32,2,1,1024]{4,0,2,1,3:T(2,128)(2,1)} %bitcast.12) | data formatting | bytes 524288 | tf_op jit(solution)/shard_map/all_to_all | solution.py:73
  62.4 1.1 %convolution_bitcast_fusion.2 = f32[2,256,32]{1,2,0:T(8,128)} fusion(bf16[2,256,1024]{2,1,0:T(8,128)(2,1)S(1)} %copy-done.2, bf16[2,2,32,1,1024]{4,2,1,3,0:T(8,128)(2,1)S(1)} %bitcast.103), kind=kOutput, calls=%fused_computation.39 | convolution fusion | flops 33554432 | bytes 1245184 | tf_op jit(solution)/shard_map/btd,bed->bte/dot_general | solution.py:76
  63.4 1.1 %convolution_bitcast_fusion.1 = f32[2,256,32]{1,2,0:T(8,128)} fusion(bf16[2,256,1024]{2,1,0:T(8,128)(2,1)S(1)} %copy-done, bf16[2,2,32,1,1024]{4,2,1,3,0:T(8,128)(2,1)S(1)} %bitcast.104), kind=kOutput, calls=%fused_computation.38 | convolution fusion | flops 33554432 | bytes 1245184 | tf_op jit(solution)/shard_map/btd,bed->bte/dot_general | solution.py:80
  64.5 1.2 %fusion.54 = f32[2,256,1024]{2,1,0:T(8,128)S(1)} fusion(bf16[2,2,32,1,1024]{4,2,1,3,0:T(8,128)(2,1)S(1)} %bitcast.105, f32[2,32]{1,0:T(2,128)} %copy-done.5, f32[2,256,32]{1,2,0:T(8,128)S(1)} %fusion.44), kind=kOutput, calls=%fused_computation.62 | convolution fusion | flops 33603904 | bytes 2359552 | tf_op jit(solution)/shard_map/bte,bed->btd/dot_general | solution.py:88
  65.7 0.0 copy-start.4
  65.7 1.1 %fusion.43 = f32[2,256,32]{1,2,0:T(8,128)S(1)} fusion(f32[2,256,32]{1,2,0:T(8,128)} %convolution_bitcast_fusion.1, f32[2,256,32]{1,2,0:T(8,128)} %get-tuple-element.17, f32[2,32]{1,0:T(2,128)} %copy-done.5), kind=kOutput, calls=%fused_computation.37 | output fusion | flops 82239 | bytes 196864 | tf_op jit(solution)/shard_map/sub | solution.py:84
  66.9 1.4 %multiply_reduce_fusion.1 = (f32[32]{0:T(128)S(1)}, f32[1024,32]{0,1:T(8,128)S(1)}) fusion(bf16[1024,32]{0,1:T(8,128)(2,1)S(1)} %multiply_convert_fusion.1, bf16[2,256,1024]{2,1,0:T(8,128)(2,1)S(1)} %copy-done, f32[2,256,32]{1,2,0:T(8,128)S(1)} %fusion.43, f32[2,256,32]{1,2,0:T(8,128)} %convolution_bitcast_fusion.2, f32[2,256,32]{1,2,0:T(8,128)} %get-tuple-element.15, ...), kind=kOutput, calls=%fused_computation.57 | convolution fusion | flops 33784320 | bytes 1443968 | tf_op jit(solution)/shard_map/btd,bte->de/dot_general | solution.py:91
  68.2 1.0 %reshape.36 = f32[32,32,32]{1,0,2:T(8,128)} reshape(f32[1024,32]{0,1:T(8,128)S(1)} %get-tuple-element.19) | data formatting | bytes 262144 | tf_op jit(solution)/shard_map/reshape | solution.py:95
  69.2 1.3 %copy.28 = f32[32,32,32]{1,2,0:T(8,128)S(1)} copy(f32[32,32,32]{1,0,2:T(8,128)} %reshape.36) | data formatting | bytes 262144 | tf_op jit(solution)/shard_map/reshape | solution.py:95
  70.6 0.1 broadcast_in_dim.14
  70.7 1.0 %fusion.73 = f32[32,32,33]{2,1,0:T(8,128)} fusion(f32[32,1,32]{1,2,0:T(8,128)S(1)} %broadcast_in_dim.14, f32[32,32,32]{1,2,0:T(8,128)S(1)} %copy.28), kind=kLoop, calls=%fused_computation.86 | loop fusion | flops 33792 | bytes 270336
  71.7 2.3 %reshape.42 = f32[32,1,1056]{2,1,0:T(1,128)} reshape(f32[32,32,33]{2,1,0:T(8,128)} %fusion.73) | data formatting | bytes 270336
  74.0 3.0 %all-to-all-start.3 = ((f32[32,1,1056]{2,1,0:T(1,128)}), f32[32,1,1056]{2,1,0:T(1,128)S(1)}, u32[]{:S(2)}, u32[]{:S(2)}) async-start(f32[32,1,1056]{2,1,0:T(1,128)} %reshape.42), calls=%async_computation.3 | async-start | bytes 294912 | tf_op jit(solution)/shard_map/all_to_all | solution.py:101
  77.0 2.4 %add_convert_fusion = bf16[2,256,1024]{2,1,0:T(8,128)(2,1)} fusion(f32[2,256,1024]{2,1,0:T(8,128)S(1)} %fusion.54, f32[2,256,32]{1,2,0:T(8,128)S(1)} %fusion.43, f32[2,256,32]{1,2,0:T(8,128)} %convolution_bitcast_fusion.2, bf16[1024,32]{0,1:T(8,128)(2,1)S(1)} %multiply_convert_fusion.1, f32[2,256,32]{1,2,0:T(8,128)} %get-tuple-element.15, ...), kind=kOutput, calls=%fused_computation.18 | convolution fusion | flops 34734624 | bytes 3409920 | tf_op jit(solution)/shard_map/bte,de->btd/dot_general | solution.py:89
  79.4 6.0 %all-to-all-done.3 = f32[32,1,1056]{2,1,0:T(1,128)S(1)} async-done(((f32[32,1,1056]{2,1,0:T(1,128)}), f32[32,1,1056]{2,1,0:T(1,128)S(1)}, u32[]{:S(2)}, u32[]{:S(2)}) %all-to-all-start.3) | async-done | bytes 135200 | tf_op jit(solution)/shard_map/all_to_all | solution.py:101
  85.4 1.0 %reduce.4 = f32[32,1056]{1,0:T(8,128)S(1)} reduce(f32[32,1,1056]{2,1,0:T(1,128)S(1)} %all-to-all-done.3, f32[]{:T(128)} %broadcast.32), dimensions={1}, to_apply=%all_to_all.35.reduce_sub_computation | reduce | bytes 270340 | tf_op jit(solution)/shard_map/all_to_all | solution.py:101
  86.4 0.6 reshape.43
  87.0 0.1 bitcast_reduce_fusion
  87.1 0.2 slice_reduce_fusion
  87.3 0.1 fusion.61
  87.3 0.7 copy.31
  (15 shorter events, 0.1 us)
Async XLA Ops:
  0.6 19.1 %copy-start = (bf16[2,256,1024]{2,1,0:T(8,128)(2,1)S(1)}, bf16[2,256,1024]{2,1,0:T(8,128)(2,1)}, u32[]{:S(2)}) copy-start(bf16[2,256,1024]{2,1,0:T(8,128)(2,1)} %param.5) | copy-start | bytes 3145732
  0.6 21.2 %copy-start.1 = (bf16[2,256,1024]{2,1,0:T(8,128)(2,1)S(1)}, bf16[2,256,1024]{2,1,0:T(8,128)(2,1)}, u32[]{:S(2)}) copy-start(bf16[2,256,1024]{2,1,0:T(8,128)(2,1)} %param.9) | copy-start | bytes 3145732
  19.1 0.6 copy-start.6
  20.9 1.0 %copy-start.5 = (f32[2,32]{1,0:T(2,128)}, f32[2,32]{1,0:T(2,128)S(1)}, u32[]{:S(2)}) copy-start(f32[2,32]{1,0:T(2,128)S(1)} %get-tuple-element.16) | copy-start | bytes 772
  21.5 13.6 %copy-start.3 = (f32[2,256]{1,0:T(2,128)}, f32[2,256]{1,0:T(2,128)S(1)}, u32[]{:S(2)}) copy-start(f32[2,256]{1,0:T(2,128)S(1)} %get-tuple-element.14) | copy-start | bytes 6148
  35.1 7.8 %slice-start = ((s8[5242880]{0:T(1024)(128)(4,1)}), s8[1048576]{0:T(1024)(128)(4,1)S(1)}, s32[]{:S(2)}) async-start(s8[5242880]{0:T(1024)(128)(4,1)} %bitcast.98), calls=%async_computation.4 | async-start | bytes 2097152
  35.2 7.8 %slice-start.1 = ((s8[5242880]{0:T(1024)(128)(4,1)}), s8[4194304]{0:T(1024)(128)(4,1)S(1)}, s32[]{:S(2)}) async-start(s8[5242880]{0:T(1024)(128)(4,1)} %bitcast.98), calls=%async_computation.5 | async-start | bytes 8388608
  35.2 9.5 %slice-start.2 = ((s8[5242880]{0:T(1024)(128)(4,1)}), s8[4194304]{0:T(1024)(128)(4,1)S(1)}, s32[]{:S(2)}) async-start(s8[5242880]{0:T(1024)(128)(4,1)} %bitcast.100), calls=%async_computation.6 | async-start | bytes 8388608
  38.9 5.8 %slice-start.3 = ((s8[5242880]{0:T(1024)(128)(4,1)}), s8[1048576]{0:T(1024)(128)(4,1)S(1)}, s32[]{:S(2)}) async-start(s8[5242880]{0:T(1024)(128)(4,1)} %bitcast.100), calls=%async_computation.7 | async-start | bytes 2097152
  47.4 13.9 %all-to-all-start.2 = ((bf16[2,64,1,1024]{3,0,2,1:T(2,128)(2,1)}), bf16[2,64,1,1024]{3,0,2,1:T(2,128)(2,1)}, u32[]{:S(2)}, u32[]{:S(2)}) async-start(bf16[2,64,1,1024]{3,0,2,1:T(2,128)(2,1)} %copy.26), calls=%async_computation.2 | async-start | bytes 524288 | tf_op jit(solution)/shard_map/all_to_all | solution.py:73
  50.9 11.4 %copy-start.2 = (bf16[2,256,1024]{2,1,0:T(8,128)(2,1)S(1)}, bf16[2,256,1024]{2,1,0:T(8,128)(2,1)}, u32[]{:S(2)}) copy-start(bf16[2,256,1024]{2,1,0:T(8,128)(2,1)} %param.9) | copy-start | bytes 3145732
  65.7 11.3 %copy-start.4 = (f32[2,256]{1,0:T(2,128)S(1)}, f32[2,256]{1,0:T(2,128)}, u32[]{:S(2)}) copy-start(f32[2,256]{1,0:T(2,128)} %copy-done.3) | copy-start | bytes 6148
  66.9 20.4 %copy-start.7 = (f32[32]{0:T(128)S(1)}, f32[32]{0:T(128)}, u32[]{:S(2)}) copy-start(f32[32]{0:T(128)} %copy-done.6) | copy-start | bytes 388
  74.0 11.5 %all-to-all-start.3 = ((f32[32,1,1056]{2,1,0:T(1,128)}), f32[32,1,1056]{2,1,0:T(1,128)S(1)}, u32[]{:S(2)}, u32[]{:S(2)}) async-start(f32[32,1,1056]{2,1,0:T(1,128)} %reshape.42), calls=%async_computation.3 | async-start | bytes 294912 | tf_op jit(solution)/shard_map/all_to_all | solution.py:101

commit v2 on v0

v2 whole, which is shorter than its diff:
```python
import functools

import jax
import jax.numpy as jnp
from jax import lax
from jax.experimental import pallas as pl
from jax.experimental.pallas import tpu as pltpu
from jax.sharding import PartitionSpec as P

LOGIT_SCALE = 2.0
EPS = 1e-06
SQRT_HALF = 0.7071067811865476
INV_ROOT = 0.3989422804014327
LANES = 128
MESH = pl.DeviceIdType.MESH
NN = (((1,), (0,)), ((), ()))
NT = (((1,), (1,)), ((), ()))
TN = (((0,), (0,)), ((), ()))
ROUTER, ROWS, GRADS, OUTS, DXS, HAT, MOMENT = range(7)


def mm(left_side, right_side, dims=NN):
    return lax.dot_general(left_side, right_side, dims, preferred_element_type=jnp.float32)


def gelu_parts(pre_value):
    cumulative = 0.5 * (1.0 + lax.erf(pre_value * SQRT_HALF))
    gelu_slope = cumulative + pre_value * jnp.exp(-0.5 * pre_value * pre_value) * INV_ROOT
    return (pre_value * cumulative, gelu_slope)


def layer_kernel(
    n, rep, tile,
    images_hbm, grad_hbm, w_in_hbm, w_out_hbm, router_ref,
    rows_ref, grads_ref, hidden_ref, pre_grad_ref, left_ref, right_ref, router_grad_ref,
    images, out_grad, w_in, w_out,
    router_all, unpacked, low_packed,
    dispatch, combine, slope, stage,
    sent_a, sent_b, sent_c, sent_d, got_a, got_b, got_c, got_d,
    hat_sent, hat_got, moment_sent, moment_got,
    load_sems, send_sems, recv_sems,
):
    local, tokens, width = images.shape
    slots = n
    chunks = width // LANES
    block = local * chunks
    pack = LANES // slots
    part = router_ref.shape[0] // pack
    hidden_width = w_in.shape[1]
    me = lax.axis_index("exp") * rep + lax.axis_index("rep")

    loads = []
    for i, (source, target) in enumerate(
        ((images_hbm, images), (grad_hbm, out_grad), (w_in_hbm.at[0], w_in), (w_out_hbm.at[0], w_out))
    ):
        loads.append(pltpu.make_async_copy(source, target, load_sems.at[i]))
        loads[-1].start()

    def place(k):
        other = lax.rem(me + k, n)
        return other, (other // rep, lax.rem(other, rep))

    barrier = pltpu.get_barrier_semaphore()

    def greet(k, carry):
        pl.semaphore_signal(barrier, inc=1, device_id=place(k)[1], device_id_type=MESH)
        return carry

    lax.fori_loop(1, n, greet, 0)

    def exchange(phase, size, source, target, whole_source=False):
        def send(k, carry):
            other, where = place(k)
            if whole_source:
                taken = source
            else:
                taken = source.at[pl.ds(pl.multiple_of(other * size, size), size)]
            pltpu.make_async_remote_copy(
                src_ref=taken,
                dst_ref=target.at[pl.ds(pl.multiple_of(me * size, size), size)],
                send_sem=send_sems.at[phase],
                recv_sem=recv_sems.at[phase],
                device_id=where,
                device_id_type=MESH,
            ).start()
            return carry

        lax.fori_loop(1, n, send, 0)

    def settle(sems, phase, size, target):
        span = target.at[pl.ds(0, (n - 1) * size)]
        pltpu.make_async_copy(span, span, sems.at[phase]).wait()

    own_parts = [router_ref[j * part : (j + 1) * part, :] for j in range(pack)]
    own_packed = own_parts[0] if pack == 1 else jnp.concatenate(own_parts, axis=1)
    own_router = pl.ds(pl.multiple_of(me * part, part), part)
    own_block = pl.ds(pl.multiple_of(me * block, block), block)
    router_all[own_router, :] = own_packed
    pl.semaphore_wait(barrier, n - 1)

    def send_router(k, carry):
        pltpu.make_async_remote_copy(
            src_ref=router_all.at[own_router],
            dst_ref=router_all.at[own_router],
            send_sem=send_sems.at[ROUTER],
            recv_sem=recv_sems.at[ROUTER],
            device_id=place(k)[1],
            device_id_type=MESH,
        ).start()
        return carry

    lax.fori_loop(1, n, send_router, 0)

    def group_sum(line):
        total = line
        for j in range(1, pack):
            total = total + pltpu.roll(line, j * slots, 1)
        return total

    settle(recv_sems, ROUTER, part, router_all)
    router_values = router_all[...]
    norm = group_sum(jnp.broadcast_to(jnp.sum(router_values * router_values, axis=0, keepdims=True), (8, LANES)))
    inv_norm = lax.rsqrt(norm + EPS)[0:1, :]
    low = (router_values * inv_norm).astype(jnp.bfloat16).astype(jnp.float32)
    low_packed[...] = low
    for j in range(pack):
        turned = low if j == 0 else pltpu.roll(low, LANES - j * slots, 1)
        unpacked[:, j * part : (j + 1) * part, :] = turned.reshape(n, part, LANES)
    router_low = jnp.transpose(unpacked[...].reshape(width, LANES))[:slots].astype(jnp.bfloat16)
    for b in range(local):
        right_ref[b, slots:, :] = router_low

    loads[0].wait()
    for b in range(local):
        logits = LOGIT_SCALE * mm(router_low, images[b], NT)
        powers = jnp.exp(logits - jnp.max(logits, axis=1, keepdims=True))
        soft = powers / jnp.sum(powers, axis=1, keepdims=True)
        dispatch[b] = soft
        soft_low = soft.astype(jnp.bfloat16)
        left_ref[b, :slots, :] = soft_low
        powers = jnp.exp(logits - jnp.max(logits, axis=0, keepdims=True))
        combine[b] = powers / jnp.sum(powers, axis=0, keepdims=True)
        slot_in = mm(soft_low, images[b])
        for c in range(chunks):
            stage[pl.ds(b * chunks + c, n, stride=block), :] = slot_in[:, c * LANES : (c + 1) * LANES]
    sent_a[...] = stage[...].astype(jnp.bfloat16)
    got_a[own_block, :] = sent_a[own_block, :]
    exchange(ROWS, block, sent_a, got_a)

    loads[1].wait()
    for b in range(local):
        slot_grad = mm(combine[b].astype(jnp.bfloat16), out_grad[b])
        for c in range(chunks):
            stage[pl.ds(b * chunks + c, n, stride=block), :] = slot_grad[:, c * LANES : (c + 1) * LANES]
    sent_b[...] = stage[...].astype(jnp.bfloat16)
    got_b[own_block, :] = sent_b[own_block, :]
    exchange(GRADS, block, sent_b, got_b)

    def gather_rows(source, target):
        stage[...] = source[...].astype(jnp.float32)
        for c in range(chunks):
            target[:, c * LANES : (c + 1) * LANES] = stage[pl.ds(c, n * local, stride=chunks), :].astype(jnp.bfloat16)

    def spread_rows(values, target, own):
        for c in range(chunks):
            stage[pl.ds(c, n * local, stride=chunks), :] = values[:, c * LANES : (c + 1) * LANES]
        target[...] = stage[...].astype(jnp.bfloat16)
        own[own_block, :] = target[own_block, :]

    loads[2].wait()
    loads[3].wait()
    settle(recv_sems, ROWS, block, got_a)
    gather_rows(got_a, rows_ref)
    slot_rows = rows_ref[...]
    total = None
    for start in range(0, hidden_width, tile):
        span = slice(start, start + tile)
        activated, gelu_slope = gelu_parts(mm(slot_rows, w_in[:, span]))
        hidden = activated.astype(jnp.bfloat16)
        hidden_ref[:, span] = hidden
        slope[:, span] = gelu_slope
        term = mm(hidden, w_out[span, :])
        total = term if total is None else total + term
    spread_rows(total, sent_c, got_c)
    exchange(OUTS, block, sent_c, got_c)

    settle(recv_sems, GRADS, block, got_b)
    gather_rows(got_b, grads_ref)
    slot_grads = grads_ref[...]
    total = None
    for start in range(0, hidden_width, tile):
        span = slice(start, start + tile)
        pre_grad = (mm(slot_grads, w_out[span, :], NT) * slope[:, span]).astype(jnp.bfloat16)
        pre_grad_ref[:, span] = pre_grad
        term = mm(pre_grad, w_in[:, span], NT)
        total = term if total is None else total + term
    spread_rows(total, sent_d, got_d)
    exchange(DXS, block, sent_d, got_d)

    def slot_values(b):
        pieces = [stage[pl.ds(b * chunks + c, n, stride=block), :] for c in range(chunks)]
        return jnp.concatenate(pieces, axis=1).astype(jnp.bfloat16)

    settle(recv_sems, OUTS, block, got_c)
    stage[...] = got_c[...].astype(jnp.float32)
    for b in range(local):
        combine_grad = mm(slot_values(b), out_grad[b], NT)
        soft = combine[b]
        combine[b] = soft * (combine_grad - jnp.sum(soft * combine_grad, axis=0, keepdims=True))

    settle(recv_sems, DXS, block, got_d)
    stage[...] = got_d[...].astype(jnp.float32)
    hat = None
    for b in range(local):
        slot_dx = slot_values(b)
        right_ref[b, :slots, :] = slot_dx
        dispatch_grad = mm(slot_dx, images[b], NT)
        soft = dispatch[b]
        grad_dispatch = soft * (dispatch_grad - jnp.sum(soft * dispatch_grad, axis=1, keepdims=True))
        logit_grad = (LOGIT_SCALE * (combine[b] + grad_dispatch)).astype(jnp.bfloat16)
        left_ref[b, slots:, :] = logit_grad
        term = mm(logit_grad, images[b])
        hat = term if hat is None else hat + term
    if slots < LANES:
        hat = jnp.concatenate((hat, jnp.zeros((LANES - slots, width), jnp.float32)), axis=0)
    unpacked[...] = jnp.transpose(hat).reshape(n, pack * part, LANES)
    packed = unpacked[:, 0:part, :].reshape(n * part, LANES)
    for j in range(1, pack):
        packed = packed + pltpu.roll(
            unpacked[:, j * part : (j + 1) * part, :].reshape(n * part, LANES), j * slots, 1
        )
    hat_sent[...] = packed
    hat_got[own_router, :] = hat_sent[own_router, :]
    exchange(HAT, part, hat_sent, hat_got)
    moment = group_sum(jnp.broadcast_to(jnp.sum(packed * low_packed[...], axis=0, keepdims=True), (8, LANES)))
    moment_sent[...] = moment[0:1, :].reshape(1, 1, LANES)
    moment_got[pl.ds(me, 1)] = moment_sent[...]
    exchange(MOMENT, 1, moment_sent, moment_got, whole_source=True)

    settle(recv_sems, HAT, part, hat_got)
    settle(recv_sems, MOMENT, 1, moment_got)
    hat_rows = jnp.sum(hat_got[...].reshape(n, part, LANES), axis=0)
    moment_whole = jnp.sum(moment_got[...], axis=0)
    own_hat = router_all[own_router, :] * inv_norm
    result = (hat_rows - own_hat * moment_whole) * inv_norm
    for j in range(pack):
        turned = result if j == 0 else pltpu.roll(result, LANES - j * slots, 1)
        router_grad_ref[j * part : (j + 1) * part, :] = turned[:, :slots]

    settle(send_sems, ROUTER, part, router_all)
    settle(send_sems, ROWS, block, sent_a)
    settle(send_sems, GRADS, block, sent_b)
    settle(send_sems, OUTS, block, sent_c)
    settle(send_sems, DXS, block, sent_d)
    settle(send_sems, HAT, part, hat_sent)
    settle(send_sems, MOMENT, 1, moment_got)


def weights_kernel(
    rows_ref, grads_ref, hidden_ref, pre_grad_ref, left_ref, right_ref,
    images_grad_ref, grad_in_ref, grad_out_ref,
):
    grad_in_ref[0] = mm(rows_ref[...], pre_grad_ref[...], TN).astype(jnp.bfloat16)
    grad_out_ref[0] = mm(hidden_ref[...], grads_ref[...], TN).astype(jnp.bfloat16)
    images_grad_ref[0] = mm(left_ref[0], right_ref[0], TN).astype(jnp.bfloat16)


def per_device(n, rep, images, router, w_in, w_out, out_grad):
    local, tokens, width = images.shape
    hidden_width = w_in.shape[2]
    slots = router.shape[1]
    images_all = local * n
    chunks = width // LANES
    block = local * chunks
    part = router.shape[0] * slots // LANES
    low, full = jnp.bfloat16, jnp.float32
    vmem = pl.BlockSpec(memory_space=pltpu.VMEM)
    anywhere = pl.BlockSpec(memory_space=pl.ANY)
    slot_rows, slot_grads, hidden, pre_grad, left, right, router_grad = pl.pallas_call(
        functools.partial(layer_kernel, n, rep, 640),
        out_shape=(
            jax.ShapeDtypeStruct((images_all, width), low),
            jax.ShapeDtypeStruct((images_all, width), low),
            jax.ShapeDtypeStruct((images_all, hidden_width), low),
            jax.ShapeDtypeStruct((images_all, hidden_width), low),
            jax.ShapeDtypeStruct((local, 2 * slots, tokens), low),
            jax.ShapeDtypeStruct((local, 2 * slots, width), low),
            jax.ShapeDtypeStruct(router.shape, full),
        ),
        in_specs=[anywhere] * 4 + [vmem],
        out_specs=(vmem,) * 7,
        scratch_shapes=[
            pltpu.VMEM((local, tokens, width), low),
            pltpu.VMEM((local, tokens, width), low),
            pltpu.VMEM((width, hidden_width), low),
            pltpu.VMEM((hidden_width, width), low),
            pltpu.VMEM((n * part, LANES), full),
            pltpu.VMEM((n, router.shape[0], LANES), full),
            pltpu.VMEM((n * part, LANES), full),
            pltpu.VMEM((local, slots, tokens), full),
            pltpu.VMEM((local, slots, tokens), full),
            pltpu.VMEM((images_all, hidden_width), full),
            pltpu.VMEM((n * block, LANES), full),
        ]
        + [pltpu.VMEM((n * block, LANES), low)] * 8
        + [
            pltpu.VMEM((n * part, LANES), full),
            pltpu.VMEM((n * part, LANES), full),
            pltpu.VMEM((1, 1, LANES), full),
            pltpu.VMEM((n, 1, LANES), full),
            pltpu.SemaphoreType.DMA((4,)),
            pltpu.SemaphoreType.DMA((7,)),
            pltpu.SemaphoreType.DMA((7,)),
        ],
        compiler_params=pltpu.CompilerParams(
            collective_id=0, has_side_effects=True, vmem_limit_bytes=48 * 1024 * 1024
        ),
        name="layer",
    )(images, out_grad, w_in, w_out, router)

    steps = 4
    tile = hidden_width // steps
    per_image = steps // local
    token_tile = tokens // per_image
    fixed = lambda i: (0, 0)
    images_grad, grad_in, grad_out = pl.pallas_call(
        weights_kernel,
        grid=(steps,),
        out_shape=(
            jax.ShapeDtypeStruct(images.shape, low),
            jax.ShapeDtypeStruct((1, width, hidden_width), low),
            jax.ShapeDtypeStruct((1, hidden_width, width), low),
        ),
        in_specs=[
            pl.BlockSpec((images_all, width), fixed),
            pl.BlockSpec((images_all, width), fixed),
            pl.BlockSpec((images_all, tile), lambda i: (0, i)),
            pl.BlockSpec((images_all, tile), lambda i: (0, i)),
            pl.BlockSpec((1, 2 * slots, token_tile), lambda i: (i // per_image, 0, i % per_image)),
            pl.BlockSpec((1, 2 * slots, width), lambda i: (i // per_image, 0, 0)),
        ],
        out_specs=(
            pl.BlockSpec((1, token_tile, width), lambda i: (i // per_image, i % per_image, 0)),
            pl.BlockSpec((1, width, tile), lambda i: (0, 0, i)),
            pl.BlockSpec((1, tile, width), lambda i: (0, i, 0)),
        ),
        compiler_params=pltpu.CompilerParams(vmem_limit_bytes=32 * 1024 * 1024),
        name="weights",
    )(slot_rows, slot_grads, hidden, pre_grad, left, right)
    return (images_grad, grad_in, grad_out, router_grad)


def solution(mesh):
    in_specs = (
        P(("exp", "rep"), None, None),
        P(("exp", "rep"), None),
        P(("exp", "rep"), None, None),
        P(("exp", "rep"), None, None),
        P(("exp", "rep"), None, None),
    )
    out_specs = (
        P(("exp", "rep"), None, None),
        P(("exp", "rep"), None, None),
        P(("exp", "rep"), None, None),
        P(("exp", "rep"), None),
    )
    rep = mesh.shape["rep"]
    n = mesh.shape["exp"] * rep
    return jax.shard_map(
        functools.partial(per_device, n, rep),
        mesh=mesh, in_specs=in_specs, out_specs=out_specs, check_vma=False,
    )
```

time: 281 us -> 50.4 us (0.18)
  waiting for transfers between devices: 144 us -> 0 us
  blocking collectives: 82 us -> 0 us
  Pallas kernels: 0 us -> 45.7 us
  matrix products: 23.2 us -> 0 us
  between operations: 14.3 us -> 0.65 us
  starting transfers between devices: 5.94 us -> 0 us
  other arithmetic: 3.6 us -> 0 us
    unnamed x2 -> x0, waiting for transfers between devices: 132 us -> none
    pallas_call x0 -> x2, Pallas kernels: none -> 45.7 us  [the longest x1 40 us: per_device(): pl.pallas_call(functools.partial(layer_kernel, n, rep, 640), out_shape=(j...]
    all_gather x1 -> x0, blocking collectives: 45.1 us -> none  [per_device(): router_whole = lax.all_gather(router, ('exp', 'rep'), axis=0, tiled=True)]
    psum x1 -> x0, blocking collectives: 36.8 us -> none  [per_device(): moment = lax.psum(jnp.sum(own_low * hat_rows, axis=0), ('exp', 'rep'))]
    dot_general x14 -> x0, matrix products: 23.2 us -> none  [the longest x2 7.84 us: contract_first(): lax.dot_general(left_side, right_side, (((0,), (0,)), ((), ())), preferre...]
    all_to_all x2 -> x0, waiting for transfers between devices: 12.5 us -> none  [the longest x1 10.5 us: per_device(): lax.all_to_all(paired, ('exp', 'rep'), split_axis=2, concat_axis=1, tiled...]
    all_to_all x2 -> x0, starting transfers between devices: 5.89 us -> none  [the longest x1 3.31 us: per_device(): lax.all_to_all(results[:, :, None, :], ('exp', 'rep'), split_axis=1, conc...]
  transfers between devices with their start and end apart: 3 -> 0, of which waited for: 3 -> 0; matrix products, arithmetic and copies ran while one was open for 4% -> 0% of each run, Pallas kernels for 0% -> 0%
where the time goes in v2:
time: 50.4 us; the launch traced here: 50.2 us
  Pallas kernels  45.7 us (91%)
  local copies, waits for them, and re-layouts  3.76 us (7%)
  between operations  0.65 us (1%)
    pallas_call x1, Pallas kernels, per_device(): pl.pallas_call(functools.partial(layer_kernel, n, rep, 640), out_shape=(j...  40 us
    pallas_call x1, Pallas kernels, per_device(): pl.pallas_call(weights_kernel, grid=(steps,), out_shape=(jax.ShapeDtypeSt...  5.75 us
    unnamed x7, local copies, waits for them, and re-layouts  3.76 us

profile of v2, /device:TPU:0, one launch (start us, length us, event | category | flops | bytes accessed | tf_op | source)
XLA Modules:
  0.0 50.2 jit_solution(11006238997037295816)
XLA Ops:
  0.6 0.0 copy-start
  0.6 1.2 %copy-done = bf16[2,256,1024]{2,1,0:T(8,128)(2,1)S(1)} copy-done((bf16[2,256,1024]{2,1,0:T(8,128)(2,1)S(1)}, bf16[2,256,1024]{2,1,0:T(8,128)(2,1)}, u32[]{:S(2)}) %copy-start) | copy-done | bytes 1048600
  1.9 0.0 copy-start.1
  1.9 1.2 %copy-done.1 = bf16[2,256,1024]{2,1,0:T(8,128)(2,1)S(1)} copy-done((bf16[2,256,1024]{2,1,0:T(8,128)(2,1)S(1)}, bf16[2,256,1024]{2,1,0:T(8,128)(2,1)}, u32[]{:S(2)}) %copy-start.1) | copy-done | bytes 1048600
  3.1 0.0 copy-start.2
  3.1 0.7 %copy-done.2 = f32[32,32]{1,0:T(8,128)S(1)} copy-done((f32[32,32]{1,0:T(8,128)S(1)}, f32[32,32]{1,0:T(8,128)}, u32[]{:S(2)}) %copy-start.2) | copy-done | bytes 4120
  3.8 40.0 %layer.1 = (bf16[64,1024]{1,0:T(8,128)(2,1)S(1)}, bf16[64,1024]{1,0:T(8,128)(2,1)S(1)}, bf16[64,2560]{1,0:T(8,128)(2,1)S(1)}, bf16[64,2560]{1,0:T(8,128)(2,1)S(1...) custom-call(bf16[2,256,1024]{2,1,0:T(8,128)(2,1)S(1)} %copy-done, ...), custom_call_target="tpu_custom_call" | custom-call | tf_op jit(solution)/shard_map/layer/pallas_call | solution.py:279
  43.8 5.8 %weights.1 = (bf16[2,256,1024]{2,1,0:T(8,128)(2,1)}, bf16[1,1024,2560]{2,1,0:T(8,128)(2,1)}, bf16[1,2560,1024]{2,1,0:T(8,128)(2,1)}) custom-call(bf16[64,1024]{1,0:T(8,128)(2,1)S(1)} %get-tuple-element.14.rows_ref, bf16[64,1024]{1,0:T(8,128)(2,1)S(1)} %get-tuple-element.15.grads_ref, bf16[64,2560]{1,0:T(8,128)(2,1)S(1)} %get-tuple-element.16.hidden_ref, ...), custom_call_target="tpu_custom_call" | custom-call | tf_op jit(solution)/shard_map/weights/pallas_call | solution.py:326
  49.6 0.6 %copy.10 = f32[32,32]{1,0:T(8,128)} copy(f32[32,32]{1,0:T(8,128)S(1)} %get-tuple-element.31) | data formatting | bytes 8192
Async XLA Ops:
  0.6 1.2 %copy-start = (bf16[2,256,1024]{2,1,0:T(8,128)(2,1)S(1)}, bf16[2,256,1024]{2,1,0:T(8,128)(2,1)}, u32[]{:S(2)}) copy-start(bf16[2,256,1024]{2,1,0:T(8,128)(2,1)} %images_hbm.1) | copy-start | bytes 3145732
  1.9 1.2 %copy-start.1 = (bf16[2,256,1024]{2,1,0:T(8,128)(2,1)S(1)}, bf16[2,256,1024]{2,1,0:T(8,128)(2,1)}, u32[]{:S(2)}) copy-start(bf16[2,256,1024]{2,1,0:T(8,128)(2,1)} %grad_hbm.1) | copy-start | bytes 3145732
  3.1 0.7 %copy-start.2 = (f32[32,32]{1,0:T(8,128)S(1)}, f32[32,32]{1,0:T(8,128)}, u32[]{:S(2)}) copy-start(f32[32,32]{1,0:T(8,128)} %router_ref.1) | copy-start | bytes 12292

commit v3 on v2

--- a/solution.py
+++ b/solution.py
@@ -31,9 +31,10 @@
 
 def layer_kernel(
     n, rep, tile,
-    images_hbm, grad_hbm, w_in_hbm, w_out_hbm, router_ref,
-    rows_ref, grads_ref, hidden_ref, pre_grad_ref, left_ref, right_ref, router_grad_ref,
-    images, out_grad, w_in, w_out,
+    images_hbm, grad_hbm, w_in_hbm, w_out_hbm, router_hbm,
+    images_grad_ref, grad_in_ref, grad_out_ref, router_grad_ref,
+    rows_ref, grads_ref, hidden_ref, pre_grad_ref, left_ref, right_ref,
+    router_ref, images, out_grad, w_in, w_out,
     router_all, unpacked, low_packed,
     dispatch, combine, slope, stage,
     sent_a, sent_b, sent_c, sent_d, got_a, got_b, got_c, got_d,
@@ -49,16 +50,31 @@
     hidden_width = w_in.shape[1]
     me = lax.axis_index("exp") * rep + lax.axis_index("rep")
 
-    loads = []
-    for i, (source, target) in enumerate(
-        ((images_hbm, images), (grad_hbm, out_grad), (w_in_hbm.at[0], w_in), (w_out_hbm.at[0], w_out))
-    ):
-        loads.append(pltpu.make_async_copy(source, target, load_sems.at[i]))
-        loads[-1].start()
+    def load(i, source, target, pieces):
+        rows = target.shape[0] // pieces
+        for k in range(pieces):
+            span = pl.ds(k * rows, rows)
+            pltpu.make_async_copy(source.at[span], target.at[span], load_sems.at[i, k]).start()
+
+    def loaded(i, source, target, pieces):
+        rows = target.shape[0] // pieces
+        for k in range(pieces):
+            span = pl.ds(k * rows, rows)
+            pltpu.make_async_copy(source.at[span], target.at[span], load_sems.at[i, k]).wait()
+
+    loads = (
+        (4, router_hbm, router_ref, 1),
+        (0, images_hbm, images, local),
+        (1, grad_hbm, out_grad, local),
+        (2, w_in_hbm.at[0], w_in, 4),
+        (3, w_out_hbm.at[0], w_out, 4),
+    )
+    for one in loads:
+        load(*one)
 
     def place(k):
         other = lax.rem(me + k, n)
-        return other, (other // rep, lax.rem(other, rep))
+        return other, (lax.div(other, rep), lax.rem(other, rep))
 
     barrier = pltpu.get_barrier_semaphore()
 
@@ -91,6 +107,7 @@
         span = target.at[pl.ds(0, (n - 1) * size)]
         pltpu.make_async_copy(span, span, sems.at[phase]).wait()
 
+    loaded(*loads[0])
     own_parts = [router_ref[j * part : (j + 1) * part, :] for j in range(pack)]
     own_packed = own_parts[0] if pack == 1 else jnp.concatenate(own_parts, axis=1)
     own_router = pl.ds(pl.multiple_of(me * part, part), part)
@@ -130,7 +147,7 @@
     for b in range(local):
         right_ref[b, slots:, :] = router_low
 
-    loads[0].wait()
+    loaded(*loads[1])
     for b in range(local):
         logits = LOGIT_SCALE * mm(router_low, images[b], NT)
         powers = jnp.exp(logits - jnp.max(logits, axis=1, keepdims=True))
@@ -147,7 +164,7 @@
     got_a[own_block, :] = sent_a[own_block, :]
     exchange(ROWS, block, sent_a, got_a)
 
-    loads[1].wait()
+    loaded(*loads[2])
     for b in range(local):
         slot_grad = mm(combine[b].astype(jnp.bfloat16), out_grad[b])
         for c in range(chunks):
@@ -167,8 +184,8 @@
         target[...] = stage[...].astype(jnp.bfloat16)
         own[own_block, :] = target[own_block, :]
 
-    loads[2].wait()
-    loads[3].wait()
+    loaded(*loads[3])
+    loaded(*loads[4])
     settle(recv_sems, ROWS, block, got_a)
     gather_rows(got_a, rows_ref)
     slot_rows = rows_ref[...]
@@ -196,6 +213,10 @@
         total = term if total is None else total + term
     spread_rows(total, sent_d, got_d)
     exchange(DXS, block, sent_d, got_d)
+
+    for start in range(0, hidden_width, tile):
+        span = slice(start, start + tile)
+        grad_out_ref[span, :] = mm(hidden_ref[:, span], slot_grads, TN).astype(jnp.bfloat16)
 
     def slot_values(b):
         pieces = [stage[pl.ds(b * chunks + c, n, stride=block), :] for c in range(chunks)]
@@ -237,6 +258,13 @@
     moment_got[pl.ds(me, 1)] = moment_sent[...]
     exchange(MOMENT, 1, moment_sent, moment_got, whole_source=True)
 
+    for b in range(local):
+        images_grad_ref[b] = mm(left_ref[b], right_ref[b], TN).astype(jnp.bfloat16)
+    rows_turned = jnp.transpose(rows_ref[...].astype(jnp.float32)).astype(jnp.bfloat16)
+    for start in range(0, hidden_width, tile):
+        span = slice(start, start + tile)
+        grad_in_ref[:, span] = mm(rows_turned, pre_grad_ref[:, span]).astype(jnp.bfloat16)
+
     settle(recv_sems, HAT, part, hat_got)
     settle(recv_sems, MOMENT, 1, moment_got)
     hat_rows = jnp.sum(hat_got[...].reshape(n, part, LANES), axis=0)
@@ -256,13 +284,18 @@
     settle(send_sems, MOMENT, 1, moment_got)
 
 
-def weights_kernel(
-    rows_ref, grads_ref, hidden_ref, pre_grad_ref, left_ref, right_ref,
-    images_grad_ref, grad_in_ref, grad_out_ref,
-):
-    grad_in_ref[0] = mm(rows_ref[...], pre_grad_ref[...], TN).astype(jnp.bfloat16)
-    grad_out_ref[0] = mm(hidden_ref[...], grads_ref[...], TN).astype(jnp.bfloat16)
-    images_grad_ref[0] = mm(left_ref[0], right_ref[0], TN).astype(jnp.bfloat16)
+def drain_kernel(pieces, *refs):
+    count = len(pieces)
+    sources, targets, sems = refs[:count], refs[count : 2 * count], refs[-1]
+    copies = []
+    for source, target, cuts in zip(sources, targets, pieces):
+        rows = source.shape[0] // cuts
+        for k in range(cuts):
+            span = pl.ds(k * rows, rows)
+            copies.append(pltpu.make_async_copy(source.at[span], target.at[span], sems.at[len(copies)]))
+            copies[-1].start()
+    for copy in copies:
+        copy.wait()
 
 
 def per_device(n, rep, images, router, w_in, w_out, out_grad):
@@ -276,20 +309,26 @@
     low, full = jnp.bfloat16, jnp.float32
     vmem = pl.BlockSpec(memory_space=pltpu.VMEM)
     anywhere = pl.BlockSpec(memory_space=pl.ANY)
-    slot_rows, slot_grads, hidden, pre_grad, left, right, router_grad = pl.pallas_call(
+    in_hbm = pl.BlockSpec(memory_space=pltpu.HBM)
+    results = (
+        jax.ShapeDtypeStruct(images.shape, low),
+        jax.ShapeDtypeStruct(w_in.shape[1:], low),
+        jax.ShapeDtypeStruct(w_out.shape[1:], low),
+        jax.ShapeDtypeStruct(router.shape, full),
+    )
+    made = pl.pallas_call(
         functools.partial(layer_kernel, n, rep, 640),
-        out_shape=(
-            jax.ShapeDtypeStruct((images_all, width), low),
-            jax.ShapeDtypeStruct((images_all, width), low),
-            jax.ShapeDtypeStruct((images_all, hidden_width), low),
-            jax.ShapeDtypeStruct((images_all, hidden_width), low),
-            jax.ShapeDtypeStruct((local, 2 * slots, tokens), low),
-            jax.ShapeDtypeStruct((local, 2 * slots, width), low),
-            jax.ShapeDtypeStruct(router.shape, full),
-        ),
-        in_specs=[anywhere] * 4 + [vmem],
-        out_specs=(vmem,) * 7,
+        out_shape=results,
+        in_specs=[in_hbm] * 5,
+        out_specs=(vmem,) * 4,
         scratch_shapes=[
+            pltpu.VMEM((images_all, width), low),
+            pltpu.VMEM((images_all, width), low),
+            pltpu.VMEM((images_all, hidden_width), low),
+            pltpu.VMEM((images_all, hidden_width), low),
+            pltpu.VMEM((local, 2 * slots, tokens), low),
+            pltpu.VMEM((local, 2 * slots, width), low),
+            pltpu.VMEM(router.shape, full),
             pltpu.VMEM((local, tokens, width), low),
             pltpu.VMEM((local, tokens, width), low),
             pltpu.VMEM((width, hidden_width), low),
@@ -308,46 +347,26 @@
             pltpu.VMEM((n * part, LANES), full),
             pltpu.VMEM((1, 1, LANES), full),
             pltpu.VMEM((n, 1, LANES), full),
-            pltpu.SemaphoreType.DMA((4,)),
+            pltpu.SemaphoreType.DMA((5, 4)),
             pltpu.SemaphoreType.DMA((7,)),
             pltpu.SemaphoreType.DMA((7,)),
         ],
         compiler_params=pltpu.CompilerParams(
-            collective_id=0, has_side_effects=True, vmem_limit_bytes=48 * 1024 * 1024
+            collective_id=0, has_side_effects=True, vmem_limit_bytes=40 * 1024 * 1024
         ),
         name="layer",
-    )(images, out_grad, w_in, w_out, router)
-
-    steps = 4
-    tile = hidden_width // steps
-    per_image = steps // local
-    token_tile = tokens // per_image
-    fixed = lambda i: (0, 0)
-    images_grad, grad_in, grad_out = pl.pallas_call(
-        weights_kernel,
-        grid=(steps,),
-        out_shape=(
-            jax.ShapeDtypeStruct(images.shape, low),
-            jax.ShapeDtypeStruct((1, width, hidden_width), low),
-            jax.ShapeDtypeStruct((1, hidden_width, width), low),
-        ),
-        in_specs=[
-            pl.BlockSpec((images_all, width), fixed),
-            pl.BlockSpec((images_all, width), fixed),
-            pl.BlockSpec((images_all, tile), lambda i: (0, i)),
-            pl.BlockSpec((images_all, tile), lambda i: (0, i)),
-            pl.BlockSpec((1, 2 * slots, token_tile), lambda i: (i // per_image, 0, i % per_image)),
-            pl.BlockSpec((1, 2 * slots, width), lambda i: (i // per_image, 0, 0)),
-        ],
-        out_specs=(
-            pl.BlockSpec((1, token_tile, width), lambda i: (i // per_image, i % per_image, 0)),
-            pl.BlockSpec((1, width, tile), lambda i: (0, 0, i)),
-            pl.BlockSpec((1, tile, width), lambda i: (0, i, 0)),
-        ),
-        compiler_params=pltpu.CompilerParams(vmem_limit_bytes=32 * 1024 * 1024),
-        name="weights",
-    )(slot_rows, slot_grads, hidden, pre_grad, left, right)
-    return (images_grad, grad_in, grad_out, router_grad)
+    )(*(pltpu.with_memory_space_constraint(x, pltpu.HBM) for x in (images, out_grad, w_in, w_out, router)))
+
+    pieces = (local, 8, 8, 1)
+    images_grad, grad_in, grad_out, router_grad = pl.pallas_call(
+        functools.partial(drain_kernel, pieces),
+        out_shape=results,
+        in_specs=[vmem] * 4,
+        out_specs=(in_hbm,) * 4,
+        scratch_shapes=[pltpu.SemaphoreType.DMA((sum(pieces),))],
+        name="drain",
+    )(*made)
+    return (images_grad, grad_in[None], grad_out[None], router_grad)
 
 
 def solution(mesh):

time: 50.4 us -> 55.3 us (1.097)
  Pallas kernels: 45.7 us -> 48.2 us
  local copies, waits for them, and re-layouts: 3.76 us -> 6.2 us
    pallas_call x2, Pallas kernels: 45.7 us -> 48.2 us  [the longest x1 39.5 us: per_device(): pl.pallas_call(functools.partial(layer_kernel, n, rep, 640), out_shape=re...]
    unnamed x7 -> x8, local copies, waits for them, and re-layouts: 3.76 us -> 6.2 us
where the time goes in v3:
time: 55.3 us; the launch traced here: 55.1 us
  Pallas kernels  48.2 us (87%)
  local copies, waits for them, and re-layouts  6.2 us (11%)
  between operations  0.65 us (1%)
    pallas_call x1, Pallas kernels, per_device(): pl.pallas_call(functools.partial(layer_kernel, n, rep, 640), out_shape=re...  39.5 us
    pallas_call x1, Pallas kernels, per_device(): pl.pallas_call(functools.partial(drain_kernel, pieces), out_shape=results...  8.76 us
    unnamed x8, local copies, waits for them, and re-layouts  6.2 us

profile of v3, /device:TPU:0, one launch (start us, length us, event | category | flops | bytes accessed | tf_op | source)
XLA Modules:
  0.0 55.1 jit_solution(16693572436805934876)
XLA Ops:
  0.6 39.5 %layer.1 = (bf16[2,256,1024]{2,1,0:T(8,128)(2,1)S(1)}, bf16[1024,2560]{1,0:T(8,128)(2,1)S(1)}, bf16[2560,1024]{1,0:T(8,128)(2,1)S(1)}, f32[32,32]{1,0:T(8,128)S(1)}) custom-call(bf16[2,256,1024]{2,1,0:T(8,128)(2,1)} %images_hbm.1, bf16[2,256,1024]{2,1,0:T(8,128)(2,1)} %grad_hbm.1, bf16[1,1024,2560]{2,1,0:T(8,128)(2,1)} %w_in_hbm.1, ...), custom_call_target="tpu_custom_call" | custom-call | tf_op jit(solution)/shard_map/layer/pallas_call | solution.py:319
  40.1 0.0 copy-start
  40.1 2.3 %copy-done = bf16[1024,2560]{1,0:T(8,128)(2,1)} copy-done((bf16[1024,2560]{1,0:T(8,128)(2,1)}, bf16[1024,2560]{1,0:T(8,128)(2,1)S(1)}, u32[]{:S(2)}) %copy-start) | copy-done | bytes 5242904
  42.4 0.0 copy-start.1
  42.4 2.3 %copy-done.1 = bf16[2560,1024]{1,0:T(8,128)(2,1)} copy-done((bf16[2560,1024]{1,0:T(8,128)(2,1)}, bf16[2560,1024]{1,0:T(8,128)(2,1)S(1)}, u32[]{:S(2)}) %copy-start.1) | copy-done | bytes 5242904
  44.8 0.0 copy-start.2
  44.8 1.0 %copy-done.2 = bf16[2,256,1024]{2,1,0:T(8,128)(2,1)} copy-done((bf16[2,256,1024]{2,1,0:T(8,128)(2,1)}, bf16[2,256,1024]{2,1,0:T(8,128)(2,1)S(1)}, u32[]{:S(2)}) %copy-start.2) | copy-done | bytes 1048600
  45.7 0.0 copy-start.3
  45.7 0.6 %copy-done.3 = f32[32,32]{1,0:T(8,128)} copy-done((f32[32,32]{1,0:T(8,128)}, f32[32,32]{1,0:T(8,128)S(1)}, u32[]{:S(2)}) %copy-start.3) | copy-done | bytes 4120
  46.3 8.8 %drain.1 = (bf16[2,256,1024]{2,1,0:T(8,128)(2,1)}, bf16[1024,2560]{1,0:T(8,128)(2,1)}, bf16[2560,1024]{1,0:T(8,128)(2,1)}, f32[32,32]{1,0:T(8,128)}) custom-call(bf16[2,256,1024]{2,1,0:T(8,128)(2,1)} %copy-done.2, bf16[1024,2560]{1,0:T(8,128)(2,1)} %copy-done, bf16[2560,1024]{1,0:T(8,128)(2,1)} %copy-done.1, f32[32,32]{1,0:T(8,128)} %copy-done.3), custom_call_target="tpu_custom_call" | custom-call | tf_op jit(solution)/shard_map/drain/pallas_call | solution.py:361
Async XLA Ops:
  40.1 2.3 %copy-start = (bf16[1024,2560]{1,0:T(8,128)(2,1)}, bf16[1024,2560]{1,0:T(8,128)(2,1)S(1)}, u32[]{:S(2)}) copy-start(bf16[1024,2560]{1,0:T(8,128)(2,1)S(1)} %get-tuple-element.13.refs_1_) | copy-start | bytes 15728644
  42.4 2.3 %copy-start.1 = (bf16[2560,1024]{1,0:T(8,128)(2,1)}, bf16[2560,1024]{1,0:T(8,128)(2,1)S(1)}, u32[]{:S(2)}) copy-start(bf16[2560,1024]{1,0:T(8,128)(2,1)S(1)} %get-tuple-element.14.refs_2_) | copy-start | bytes 15728644
  44.8 1.0 %copy-start.2 = (bf16[2,256,1024]{2,1,0:T(8,128)(2,1)}, bf16[2,256,1024]{2,1,0:T(8,128)(2,1)S(1)}, u32[]{:S(2)}) copy-start(bf16[2,256,1024]{2,1,0:T(8,128)(2,1)S(1)} %get-tuple-element.12.refs_0_) | copy-start | bytes 3145732
  45.7 0.6 %copy-start.3 = (f32[32,32]{1,0:T(8,128)}, f32[32,32]{1,0:T(8,128)S(1)}, u32[]{:S(2)}) copy-start(f32[32,32]{1,0:T(8,128)S(1)} %get-tuple-element.15.refs_3_) | copy-start | bytes 12292

commit v4 on v3

--- a/solution.py
+++ b/solution.py
@@ -12,7 +12,8 @@
 SQRT_HALF = 0.7071067811865476
 INV_ROOT = 0.3989422804014327
 LANES = 128
-MESH = pl.DeviceIdType.MESH
+LOGICAL = pl.DeviceIdType.LOGICAL
+GROUP = 8
 NN = (((1,), (0,)), ((), ()))
 NT = (((1,), (1,)), ((), ()))
 TN = (((0,), (0,)), ((), ()))
@@ -69,24 +70,36 @@
         (2, w_in_hbm.at[0], w_in, 4),
         (3, w_out_hbm.at[0], w_out, 4),
     )
-    for one in loads:
-        load(*one)
-
-    def place(k):
-        other = lax.rem(me + k, n)
-        return other, (lax.div(other, rep), lax.rem(other, rep))
+    load(*loads[0])
+
+    def each_other(act):
+        def one(base, step):
+            half = (step + 1) // 2
+            k = n // 2 + (base + half if step % 2 == 0 else -(base + half))
+            other = me + k
+            act(jnp.where(other >= n, other - n, other))
+
+        def group(g, carry):
+            for step in range(GROUP):
+                one(g * (GROUP // 2), step)
+            return carry
+
+        groups = (n - 1) // GROUP
+        lax.fori_loop(0, groups, group, 0)
+        for step in range(n - 1 - groups * GROUP):
+            one(groups * (GROUP // 2), step)
 
     barrier = pltpu.get_barrier_semaphore()
 
-    def greet(k, carry):
-        pl.semaphore_signal(barrier, inc=1, device_id=place(k)[1], device_id_type=MESH)
-        return carry
-
-    lax.fori_loop(1, n, greet, 0)
+    def greet(other):
+        pl.semaphore_signal(barrier, inc=1, device_id=other, device_id_type=LOGICAL)
+
+    each_other(greet)
+    for one_load in loads[1:]:
+        load(*one_load)
 
     def exchange(phase, size, source, target, whole_source=False):
-        def send(k, carry):
-            other, where = place(k)
+        def send(other):
             if whole_source:
                 taken = source
             else:
@@ -96,12 +109,11 @@
                 dst_ref=target.at[pl.ds(pl.multiple_of(me * size, size), size)],
                 send_sem=send_sems.at[phase],
                 recv_sem=recv_sems.at[phase],
-                device_id=where,
-                device_id_type=MESH,
+                device_id=other,
+                device_id_type=LOGICAL,
             ).start()
-            return carry
-
-        lax.fori_loop(1, n, send, 0)
+
+        each_other(send)
 
     def settle(sems, phase, size, target):
         span = target.at[pl.ds(0, (n - 1) * size)]
@@ -115,18 +127,17 @@
     router_all[own_router, :] = own_packed
     pl.semaphore_wait(barrier, n - 1)
 
-    def send_router(k, carry):
+    def send_router(other):
         pltpu.make_async_remote_copy(
             src_ref=router_all.at[own_router],
             dst_ref=router_all.at[own_router],
             send_sem=send_sems.at[ROUTER],
             recv_sem=recv_sems.at[ROUTER],
-            device_id=place(k)[1],
-            device_id_type=MESH,
+            device_id=other,
+            device_id_type=LOGICAL,
         ).start()
-        return carry
-
-    lax.fori_loop(1, n, send_router, 0)
+
+    each_other(send_router)
 
     def group_sum(line):
         total = line
@@ -361,9 +372,10 @@
     images_grad, grad_in, grad_out, router_grad = pl.pallas_call(
         functools.partial(drain_kernel, pieces),
         out_shape=results,
-        in_specs=[vmem] * 4,
+        in_specs=[anywhere] * 4,
         out_specs=(in_hbm,) * 4,
         scratch_shapes=[pltpu.SemaphoreType.DMA((sum(pieces),))],
+        compiler_params=pltpu.CompilerParams(vmem_limit_bytes=2 * 1024 * 1024),
         name="drain",
     )(*made)
     return (images_grad, grad_in[None], grad_out[None], router_grad)

time: 55.3 us -> 45.3 us (0.82)
  local copies, waits for them, and re-layouts: 6.2 us -> 0 us
  Pallas kernels: 48.2 us -> 44.5 us
    unnamed x8 -> x0, local copies, waits for them, and re-layouts: 6.2 us -> none
    pallas_call x1, Pallas kernels: 8.76 us -> 4.4 us  [per_device(): pl.pallas_call(functools.partial(drain_kernel, pieces), out_shape=results...]
    pallas_call x1, Pallas kernels: 39.5 us -> 40.1 us  [per_device(): pl.pallas_call(functools.partial(layer_kernel, n, rep, 640), out_shape=re...]
where the time goes in v4:
time: 45.3 us; the launch traced here: 45.1 us
  Pallas kernels  44.5 us (98%)
  between operations  0.64 us (1%)
    pallas_call x1, Pallas kernels, per_device(): pl.pallas_call(functools.partial(layer_kernel, n, rep, 640), out_shape=re...  40.1 us
    pallas_call x1, Pallas kernels, per_device(): pl.pallas_call(functools.partial(drain_kernel, pieces), out_shape=results...  4.4 us

profile of v4, /device:TPU:0, one launch (start us, length us, event | category | flops | bytes accessed | tf_op | source)
XLA Modules:
  0.0 45.1 jit_solution(15838247194045590429)
XLA Ops:
  0.6 40.1 %layer.1 = (bf16[2,256,1024]{2,1,0:T(8,128)(2,1)S(1)}, bf16[1024,2560]{1,0:T(8,128)(2,1)S(1)}, bf16[2560,1024]{1,0:T(8,128)(2,1)S(1)}, f32[32,32]{1,0:T(8,128)S(1)}) custom-call(bf16[2,256,1024]{2,1,0:T(8,128)(2,1)} %images_hbm.1, bf16[2,256,1024]{2,1,0:T(8,128)(2,1)} %grad_hbm.1, bf16[1,1024,2560]{2,1,0:T(8,128)(2,1)} %w_in_hbm.1, ...), custom_call_target="tpu_custom_call" | custom-call | tf_op jit(solution)/shard_map/layer/pallas_call | solution.py:330
  40.7 4.4 %drain.1 = (bf16[2,256,1024]{2,1,0:T(8,128)(2,1)}, bf16[1024,2560]{1,0:T(8,128)(2,1)}, bf16[2560,1024]{1,0:T(8,128)(2,1)}, f32[32,32]{1,0:T(8,128)}) custom-call(bf16[2,256,1024]{2,1,0:T(8,128)(2,1)S(1)} %get-tuple-element.12.refs_0_, bf16[1024,2560]{1,0:T(8,128)(2,1)S(1)} %get-tuple-element.13.refs_1_, bf16[2560,1024]{1,0:T(8,128)(2,1)S(1)} %get-tuple-element.14.refs_2_, ...), custom_call_target="tpu_custom_call" | custom-call | tf_op jit(solution)/shard_map/drain/pallas_call | solution.py:372

commit v5 on v4

--- a/solution.py
+++ b/solution.py
@@ -31,7 +31,7 @@
 
 
 def layer_kernel(
-    n, rep, tile,
+    n, tile,
     images_hbm, grad_hbm, w_in_hbm, w_out_hbm, router_hbm,
     images_grad_ref, grad_in_ref, grad_out_ref, router_grad_ref,
     rows_ref, grads_ref, hidden_ref, pre_grad_ref, left_ref, right_ref,
@@ -49,7 +49,7 @@
     pack = LANES // slots
     part = router_ref.shape[0] // pack
     hidden_width = w_in.shape[1]
-    me = lax.axis_index("exp") * rep + lax.axis_index("rep")
+    me = lax.axis_index("exp") * lax.axis_size("rep") + lax.axis_index("rep")
 
     def load(i, source, target, pieces):
         rows = target.shape[0] // pieces
@@ -166,8 +166,7 @@
         dispatch[b] = soft
         soft_low = soft.astype(jnp.bfloat16)
         left_ref[b, :slots, :] = soft_low
-        powers = jnp.exp(logits - jnp.max(logits, axis=0, keepdims=True))
-        combine[b] = powers / jnp.sum(powers, axis=0, keepdims=True)
+        combine[b] = logits
         slot_in = mm(soft_low, images[b])
         for c in range(chunks):
             stage[pl.ds(b * chunks + c, n, stride=block), :] = slot_in[:, c * LANES : (c + 1) * LANES]
@@ -177,7 +176,11 @@
 
     loaded(*loads[2])
     for b in range(local):
-        slot_grad = mm(combine[b].astype(jnp.bfloat16), out_grad[b])
+        logits = combine[b]
+        powers = jnp.exp(logits - jnp.max(logits, axis=0, keepdims=True))
+        soft = powers / jnp.sum(powers, axis=0, keepdims=True)
+        combine[b] = soft
+        slot_grad = mm(soft.astype(jnp.bfloat16), out_grad[b])
         for c in range(chunks):
             stage[pl.ds(b * chunks + c, n, stride=block), :] = slot_grad[:, c * LANES : (c + 1) * LANES]
     sent_b[...] = stage[...].astype(jnp.bfloat16)
@@ -328,7 +331,7 @@
         jax.ShapeDtypeStruct(router.shape, full),
     )
     made = pl.pallas_call(
-        functools.partial(layer_kernel, n, rep, 640),
+        functools.partial(layer_kernel, n, 512),
         out_shape=results,
         in_specs=[in_hbm] * 5,
         out_specs=(vmem,) * 4,

time: 45.3 us -> 45.7 us (level)
  no operation moved by 1% of the time
where the time goes in v5:
time: 45.7 us; the launch traced here: 45.4 us
  Pallas kernels  44.8 us (98%)
  between operations  0.64 us (1%)
    pallas_call x1, Pallas kernels, per_device(): pl.pallas_call(functools.partial(layer_kernel, n, 512), out_shape=results...  40.4 us
    pallas_call x1, Pallas kernels, per_device(): pl.pallas_call(functools.partial(drain_kernel, pieces), out_shape=results...  4.4 us

profile of v5, /device:TPU:0, one launch (start us, length us, event | category | flops | bytes accessed | tf_op | source)
XLA Modules:
  0.0 45.4 jit_solution(9122205270086514418)
XLA Ops:
  0.6 40.4 %layer.1 = (bf16[2,256,1024]{2,1,0:T(8,128)(2,1)S(1)}, bf16[1024,2560]{1,0:T(8,128)(2,1)S(1)}, bf16[2560,1024]{1,0:T(8,128)(2,1)S(1)}, f32[32,32]{1,0:T(8,128)S(1)}) custom-call(bf16[2,256,1024]{2,1,0:T(8,128)(2,1)} %images_hbm.1, bf16[2,256,1024]{2,1,0:T(8,128)(2,1)} %grad_hbm.1, bf16[1,1024,2560]{2,1,0:T(8,128)(2,1)} %w_in_hbm.1, ...), custom_call_target="tpu_custom_call" | custom-call | tf_op jit(solution)/shard_map/layer/pallas_call | solution.py:333
  41.0 4.4 %drain.1 = (bf16[2,256,1024]{2,1,0:T(8,128)(2,1)}, bf16[1024,2560]{1,0:T(8,128)(2,1)}, bf16[2560,1024]{1,0:T(8,128)(2,1)}, f32[32,32]{1,0:T(8,128)}) custom-call(bf16[2,256,1024]{2,1,0:T(8,128)(2,1)S(1)} %get-tuple-element.12.refs_0_, bf16[1024,2560]{1,0:T(8,128)(2,1)S(1)} %get-tuple-element.13.refs_1_, bf16[2560,1024]{1,0:T(8,128)(2,1)S(1)} %get-tuple-element.14.refs_2_, ...), custom_call_target="tpu_custom_call" | custom-call | tf_op jit(solution)/shard_map/drain/pallas_call | solution.py:375

commit v6 on v5

--- a/solution.py
+++ b/solution.py
@@ -17,7 +17,7 @@
 NN = (((1,), (0,)), ((), ()))
 NT = (((1,), (1,)), ((), ()))
 TN = (((0,), (0,)), ((), ()))
-ROUTER, ROWS, GRADS, OUTS, DXS, HAT, MOMENT = range(7)
+ROUTER, ROWS, GRADS, OUTS, DXS, HAT, MOMENT, COLUMN = range(8)
 
 
 def mm(left_side, right_side, dims=NN):
@@ -49,7 +49,9 @@
     pack = LANES // slots
     part = router_ref.shape[0] // pack
     hidden_width = w_in.shape[1]
-    me = lax.axis_index("exp") * lax.axis_size("rep") + lax.axis_index("rep")
+    exps, reps = unpacked.shape[0], unpacked.shape[1]
+    my_exp, my_rep = lax.axis_index("exp"), lax.axis_index("rep")
+    me = my_exp * reps + my_rep
 
     def load(i, source, target, pieces):
         rows = target.shape[0] // pieces
@@ -124,20 +126,32 @@
     own_packed = own_parts[0] if pack == 1 else jnp.concatenate(own_parts, axis=1)
     own_router = pl.ds(pl.multiple_of(me * part, part), part)
     own_block = pl.ds(pl.multiple_of(me * block, block), block)
-    router_all[own_router, :] = own_packed
+    own_tile = pl.ds(pl.multiple_of((my_rep * exps + my_exp) * part, part), part)
+    own_column = pl.ds(pl.multiple_of(my_rep * exps * part, exps * part), exps * part)
+    router_all[own_tile, :] = own_packed
     pl.semaphore_wait(barrier, n - 1)
 
-    def send_router(other):
+    def send_router(span, phase, other):
         pltpu.make_async_remote_copy(
-            src_ref=router_all.at[own_router],
-            dst_ref=router_all.at[own_router],
-            send_sem=send_sems.at[ROUTER],
-            recv_sem=recv_sems.at[ROUTER],
+            src_ref=router_all.at[span],
+            dst_ref=router_all.at[span],
+            send_sem=send_sems.at[phase],
+            recv_sem=recv_sems.at[phase],
             device_id=other,
             device_id_type=LOGICAL,
         ).start()
 
-    each_other(send_router)
+    def router_done(sems, phase, rows):
+        span = router_all.at[pl.ds(0, rows)]
+        pltpu.make_async_copy(span, span, sems.at[phase]).wait()
+
+    tile_rows, column_rows = (exps - 1) * part, (reps - 1) * exps * part
+    for k in range(1, exps):
+        send_router(own_tile, ROUTER, lax.rem(my_exp + k, exps) * reps + my_rep)
+    router_done(recv_sems, ROUTER, tile_rows)
+    for k in range(1, reps):
+        send_router(own_column, COLUMN, my_exp * reps + lax.rem(my_rep + k, reps))
+    router_done(recv_sems, COLUMN, column_rows)
 
     def group_sum(line):
         total = line
@@ -145,15 +159,17 @@
             total = total + pltpu.roll(line, j * slots, 1)
         return total
 
-    settle(recv_sems, ROUTER, part, router_all)
     router_values = router_all[...]
     norm = group_sum(jnp.broadcast_to(jnp.sum(router_values * router_values, axis=0, keepdims=True), (8, LANES)))
     inv_norm = lax.rsqrt(norm + EPS)[0:1, :]
     low = (router_values * inv_norm).astype(jnp.bfloat16).astype(jnp.float32)
-    low_packed[...] = low
+    for q in range(reps):
+        low_packed[:, q] = low.reshape(reps, exps, part, LANES)[q]
     for j in range(pack):
         turned = low if j == 0 else pltpu.roll(low, LANES - j * slots, 1)
-        unpacked[:, j * part : (j + 1) * part, :] = turned.reshape(n, part, LANES)
+        turned = turned.reshape(reps, exps, part, LANES)
+        for q in range(reps):
+            unpacked[:, q, j * part : (j + 1) * part, :] = turned[q]
     router_low = jnp.transpose(unpacked[...].reshape(width, LANES))[:slots].astype(jnp.bfloat16)
     for b in range(local):
         right_ref[b, slots:, :] = router_low
@@ -258,16 +274,16 @@
         hat = term if hat is None else hat + term
     if slots < LANES:
         hat = jnp.concatenate((hat, jnp.zeros((LANES - slots, width), jnp.float32)), axis=0)
-    unpacked[...] = jnp.transpose(hat).reshape(n, pack * part, LANES)
-    packed = unpacked[:, 0:part, :].reshape(n * part, LANES)
+    unpacked[...] = jnp.transpose(hat).reshape(exps, reps, pack * part, LANES)
+    packed = unpacked[:, :, 0:part, :].reshape(n * part, LANES)
     for j in range(1, pack):
         packed = packed + pltpu.roll(
-            unpacked[:, j * part : (j + 1) * part, :].reshape(n * part, LANES), j * slots, 1
+            unpacked[:, :, j * part : (j + 1) * part, :].reshape(n * part, LANES), j * slots, 1
         )
     hat_sent[...] = packed
     hat_got[own_router, :] = hat_sent[own_router, :]
     exchange(HAT, part, hat_sent, hat_got)
-    moment = group_sum(jnp.broadcast_to(jnp.sum(packed * low_packed[...], axis=0, keepdims=True), (8, LANES)))
+    moment = group_sum(jnp.broadcast_to(jnp.sum(packed * low_packed[...].reshape(n * part, LANES), axis=0, keepdims=True), (8, LANES)))
     moment_sent[...] = moment[0:1, :].reshape(1, 1, LANES)
     moment_got[pl.ds(me, 1)] = moment_sent[...]
     exchange(MOMENT, 1, moment_sent, moment_got, whole_source=True)
@@ -283,13 +299,14 @@
     settle(recv_sems, MOMENT, 1, moment_got)
     hat_rows = jnp.sum(hat_got[...].reshape(n, part, LANES), axis=0)
     moment_whole = jnp.sum(moment_got[...], axis=0)
-    own_hat = router_all[own_router, :] * inv_norm
+    own_hat = router_all[own_tile, :] * inv_norm
     result = (hat_rows - own_hat * moment_whole) * inv_norm
     for j in range(pack):
         turned = result if j == 0 else pltpu.roll(result, LANES - j * slots, 1)
         router_grad_ref[j * part : (j + 1) * part, :] = turned[:, :slots]
 
-    settle(send_sems, ROUTER, part, router_all)
+    router_done(send_sems, ROUTER, tile_rows)
+    router_done(send_sems, COLUMN, column_rows)
     settle(send_sems, ROWS, block, sent_a)
     settle(send_sems, GRADS, block, sent_b)
     settle(send_sems, OUTS, block, sent_c)
@@ -348,8 +365,8 @@
             pltpu.VMEM((width, hidden_width), low),
             pltpu.VMEM((hidden_width, width), low),
             pltpu.VMEM((n * part, LANES), full),
-            pltpu.VMEM((n, router.shape[0], LANES), full),
-            pltpu.VMEM((n * part, LANES), full),
+            pltpu.VMEM((n // rep, rep, router.shape[0], LANES), full),
+            pltpu.VMEM((n // rep, rep, part, LANES), full),
             pltpu.VMEM((local, slots, tokens), full),
             pltpu.VMEM((local, slots, tokens), full),
             pltpu.VMEM((images_all, hidden_width), full),
@@ -362,8 +379,8 @@
             pltpu.VMEM((1, 1, LANES), full),
             pltpu.VMEM((n, 1, LANES), full),
             pltpu.SemaphoreType.DMA((5, 4)),
-            pltpu.SemaphoreType.DMA((7,)),
-            pltpu.SemaphoreType.DMA((7,)),
+            pltpu.SemaphoreType.DMA((8,)),
+            pltpu.SemaphoreType.DMA((8,)),
         ],
         compiler_params=pltpu.CompilerParams(
             collective_id=0, has_side_effects=True, vmem_limit_bytes=40 * 1024 * 1024

time: 45.7 us -> 46.9 us (1.026)
  Pallas kernels: 44.8 us -> 46.1 us
    pallas_call x1, Pallas kernels: 40.4 us -> 41.7 us  [per_device(): pl.pallas_call(functools.partial(layer_kernel, n, 512), out_shape=results...]
where the time goes in v6:
time: 46.9 us; the launch traced here: 46.7 us
  Pallas kernels  46.1 us (98%)
  between operations  0.64 us (1%)
    pallas_call x1, Pallas kernels, per_device(): pl.pallas_call(functools.partial(layer_kernel, n, 512), out_shape=results...  41.7 us
    pallas_call x1, Pallas kernels, per_device(): pl.pallas_call(functools.partial(drain_kernel, pieces), out_shape=results...  4.4 us

profile of v6, /device:TPU:0, one launch (start us, length us, event | category | flops | bytes accessed | tf_op | source)
XLA Modules:
  0.0 46.7 jit_solution(1068733471753809244)
XLA Ops:
  0.6 41.7 %layer.1 = (bf16[2,256,1024]{2,1,0:T(8,128)(2,1)S(1)}, bf16[1024,2560]{1,0:T(8,128)(2,1)S(1)}, bf16[2560,1024]{1,0:T(8,128)(2,1)S(1)}, f32[32,32]{1,0:T(8,128)S(1)}) custom-call(bf16[2,256,1024]{2,1,0:T(8,128)(2,1)} %images_hbm.1, bf16[2,256,1024]{2,1,0:T(8,128)(2,1)} %grad_hbm.1, bf16[1,1024,2560]{2,1,0:T(8,128)(2,1)} %w_in_hbm.1, ...), custom_call_target="tpu_custom_call" | custom-call | tf_op jit(solution)/shard_map/layer/pallas_call | solution.py:350
  42.3 4.4 %drain.1 = (bf16[2,256,1024]{2,1,0:T(8,128)(2,1)}, bf16[1024,2560]{1,0:T(8,128)(2,1)}, bf16[2560,1024]{1,0:T(8,128)(2,1)}, f32[32,32]{1,0:T(8,128)}) custom-call(bf16[2,256,1024]{2,1,0:T(8,128)(2,1)S(1)} %get-tuple-element.12.refs_0_, bf16[1024,2560]{1,0:T(8,128)(2,1)S(1)} %get-tuple-element.13.refs_1_, bf16[2560,1024]{1,0:T(8,128)(2,1)S(1)} %get-tuple-element.14.refs_2_, ...), custom_call_target="tpu_custom_call" | custom-call | tf_op jit(solution)/shard_map/drain/pallas_call | solution.py:392
